TPU v7x, 32 devices: a whole 2x2x4 slice. The times are simulated.
32 devices in a mesh: depth: 4 (over z), rows: 8 (over y, x, core).
Axes of the slice: x: 2, y: 2, z: 4, core: 2. Of those that a mesh axis runs over, the one named last changes fastest.
Arguments:
- node_feat: bfloat16 [512, 8192], P('depth', 'rows'), may hold values from -6 to 6
- grad_out: bfloat16 [512, 8192], P('depth', 'rows'), may hold values from -0.25 to 0.25
- adjacency: bfloat16 [128, 256, 256], P('rows'), may hold values from -0.1875 to 0.1875
- tile_count: int32 [8], replicated, may hold values from 4 to 16, as said below
- tile_row: int32 [8, 16], replicated, may hold values from 0 to 3, as said below
- tile_col: int32 [8, 16], replicated, may hold values from 0 to 31, as said below
Outputs:
- weight_grad: float32 [8, 16, 256, 256], P('rows', 'depth')
Inputs may be any that keep to these rules, and one draw needn't show every extreme that they name: `tile_count`: the number of live slots of each owner; one owner has exactly 16 in every draw. `tile_row`: 0 in dead slots. `tile_col`: 0 in dead slots. An owner's live slots name distinct column tiles; at most 2 of them lie among the node tiles of any one owner (column tile // 4), and every owner has exactly 2 from some owner.
All inputs are finite; a program needn't handle non-finite values.
Results may differ from a plain program's by a relative error of at most 0.0029.
Values may be sent and summed in bfloat16 or wider, within the bound.
A program may use at most 64 MiB of HBM per device.

v0:
```python
import jax
import jax.numpy as jnp
from jax import lax
from jax.sharding import PartitionSpec as P

PAIR_MOST = 2


top_precision = lax.Precision.HIGHEST


def slot_tables(tile_row, tile_col, tile_count, row_tiles, pair_most, own_index):
    slot_count = tile_col.shape[1]
    slot_ids = jnp.arange(slot_count, dtype=jnp.int32)
    is_live = slot_ids[None, :] < tile_count[:, None]
    owners = tile_col // row_tiles
    earlier = slot_ids[:, None] > slot_ids[None, :]
    same_owner = (
        (owners[:, :, None] == owners[:, None, :]) & is_live[:, None, :] & earlier[None, :, :]
    )
    rank_of = jnp.sum(same_owner.astype(jnp.int32), axis=2)
    buffer_pos = owners * pair_most + rank_of
    wanted = is_live & (owners == own_index)
    rank_ids = jnp.arange(pair_most, dtype=jnp.int32)
    matched = wanted[:, :, None] & (rank_of[:, :, None] == rank_ids[None, None, :])
    local_tile = jnp.sum(jnp.where(matched, (tile_col % row_tiles)[:, :, None], 0), axis=1).reshape(
        -1
    )
    send_valid = jnp.any(matched, axis=1).reshape(-1)
    my_pos = jnp.take(buffer_pos, own_index, axis=0)
    my_live = jnp.take(is_live, own_index, axis=0)
    my_row = jnp.take(tile_row, own_index, axis=0)
    return (my_pos, my_live, my_row, local_tile, send_valid)


def pick_tiles(source, indices, keep):
    picked = jnp.take(source, indices, axis=1)
    return jnp.where(keep[None, :, None], picked, jnp.zeros((), source.dtype))


def body(node_feat, grad_out, adjacency, tile_count, tile_row, tile_col):
    tile_width = adjacency.shape[1]
    feat_part = node_feat.shape[0]
    row_tiles = node_feat.shape[1] // tile_width
    pair_most = PAIR_MOST
    peer_count = lax.axis_size("rows")
    own_index = lax.axis_index("rows")
    my_pos, my_live, my_row, local_tile, send_valid = slot_tables(
        tile_row, tile_col, tile_count, row_tiles, pair_most, own_index
    )
    buffer_len = peer_count * pair_most
    feat_tiles = node_feat.reshape(feat_part, row_tiles, tile_width)
    grad_tiles = grad_out.reshape(feat_part, row_tiles, tile_width)
    outgoing = pick_tiles(feat_tiles, local_tile, send_valid)
    incoming = lax.all_to_all(outgoing, "rows", split_axis=1, concat_axis=1, tiled=True)
    x_cols = pick_tiles(incoming, my_pos, my_live)
    dy_rows = jnp.take(grad_tiles, my_row, axis=1)
    g_terms = jnp.einsum("fsa,sab->fsb", dy_rows, adjacency, preferred_element_type=jnp.float32)
    placing = (
        (my_pos[:, None] == jnp.arange(buffer_len, dtype=jnp.int32)[None, :]) & my_live[:, None]
    ).astype(jnp.float32)
    g_outgoing = jnp.einsum("fsb,sp->fpb", g_terms, placing, precision=top_precision)
    g_incoming = lax.all_to_all(g_outgoing, "rows", split_axis=1, concat_axis=1, tiled=True)
    tile_ids = jnp.arange(row_tiles, dtype=jnp.int32)
    col_onehot = ((local_tile[:, None] == tile_ids[None, :]) & send_valid[:, None]).astype(
        jnp.float32
    )
    summed_g = jnp.einsum("fpb,pr->frb", g_incoming, col_onehot, precision=top_precision).astype(
        jnp.bfloat16
    )
    h_terms = jnp.einsum("fsb,sab->fsa", x_cols, adjacency, preferred_element_type=jnp.float32)
    row_onehot = ((my_row[:, None] == tile_ids[None, :]) & my_live[:, None]).astype(jnp.float32)
    summed_h = jnp.einsum("fsa,sr->fra", h_terms, row_onehot, precision=top_precision).astype(
        jnp.bfloat16
    )
    h_outgoing = pick_tiles(summed_h, local_tile, send_valid)
    h_incoming = lax.all_to_all(h_outgoing, "rows", split_axis=1, concat_axis=1, tiled=True)
    h_cols = pick_tiles(h_incoming, my_pos, my_live)
    g_rows = jnp.take(summed_g, my_row, axis=1)
    partial_value = jnp.einsum("fsa,fsb->sab", dy_rows, h_cols, preferred_element_type=jnp.float32)
    partial_value = partial_value + jnp.einsum(
        "fsa,fsb->sab", g_rows, x_cols, preferred_element_type=jnp.float32
    )
    result = lax.psum_scatter(partial_value, "depth", scatter_dimension=0, tiled=True)
    return result[None]


def solution(mesh):
    in_specs = (P("depth", "rows"), P("depth", "rows"), P("rows", None, None), P(), P(), P())
    out_specs = P("rows", "depth", None, None)
    return jax.shard_map(body, mesh=mesh, in_specs=in_specs, out_specs=out_specs, check_vma=False)
```

profile of v0, /device:TPU:18, one launch (start us, length us, event | category | flops | bytes accessed | tf_op | source)
XLA Modules:
  0.0 175.3 jit_solution(17038885295798893254)
XLA Ops:
  6.5 0.0 copy-start
  6.5 0.8 add_select_fusion
  7.4 0.8 compare_and_fusion
  8.2 0.3 convert_reduce_fusion
  8.5 0.2 fusion.34
  8.6 0.2 select_reduce_fusion
  8.8 0.1 copy.46
  8.9 0.1 broadcast_in_dim.99
  8.9 0.1 copy.47
  9.0 0.1 reshape.67
  9.1 0.7 compare_and_fusion.3
  9.9 1.1 copy.48
  11.0 0.1 copy.49
  11.1 0.6 gather_fusion.1
  11.8 0.0 copy-start.3
  11.8 1.2 bitcast_select_fusion.4
  13.0 4.6 %all-to-all-start = ((bf16[128,16,256]{2,0,1:T(8,128)(2,1)}), bf16[128,16,256]{2,0,1:T(8,128)(2,1)}, u32[]{:S(2)}, u32[]{:S(2)}) async-start(bf16[128,16,256]{2,0,1:T(8,128)(2,1)} %bitcast_select_fusion.4), calls=%async_computation | async-start | bytes 2097152 | tf_op jit(solution)/shard_map/all_to_all | solution.py:55
  17.6 0.0 copy-done.3
  17.6 0.2 copy.44
  17.8 0.1 copy.45
  18.0 0.6 gather_fusion
  18.6 0.0 copy-done
  18.6 0.5 convolution_bitcast_fusion
  19.1 2.3 %fusion.6 = f32[128,16,256]{2,1,0:T(8,128)S(1)} fusion(f32[128,16,256]{2,0,1:T(8,128)S(1)} %convolution_bitcast_fusion, s32[16]{0:T(128)S(1)} %get-tuple-element.33, pred[16]{0:T(512)(128)(4,1)S(1)} %select_bitcast_fusion), kind=kOutput, calls=%fused_computation.13 | convolution fusion | flops 100663808 | bytes 4194384 | tf_op jit(solution)/shard_map/fsb,sp->fpb/dot_general | solution.py:62
  21.5 2.5 %copy.54 = f32[128,16,256]{2,0,1:T(8,128)} copy(f32[128,16,256]{2,1,0:T(8,128)S(1)} %fusion.6) | data formatting | bytes 4194304 | tf_op jit(solution)/shard_map/fsb,sp->fpb/transpose | solution.py:62
  24.0 7.6 %all-to-all-done = bf16[128,16,256]{2,0,1:T(8,128)(2,1)} async-done(((bf16[128,16,256]{2,0,1:T(8,128)(2,1)}), bf16[128,16,256]{2,0,1:T(8,128)(2,1)}, u32[]{:S(2)}, u32[]{:S(2)}) %all-to-all-start) | async-done | bytes 1048608 | tf_op jit(solution)/shard_map/all_to_all | solution.py:55
  31.6 5.7 %all-to-all-start.2 = ((f32[128,16,256]{2,0,1:T(8,128)}), f32[128,16,256]{2,0,1:T(8,128)}, u32[]{:S(2)}, u32[]{:S(2)}) async-start(f32[128,16,256]{2,0,1:T(8,128)} %copy.54), calls=%async_computation.2 | async-start | bytes 4194304 | tf_op jit(solution)/shard_map/all_to_all | solution.py:63
  37.4 2.8 %gather_fusion.2 = bf16[16,128,256]{2,1,0:T(8,128)(2,1)} fusion(bf16[128,16,256]{2,0,1:T(8,128)(2,1)} %all-to-all-done, s32[1024]{0:T(1024)S(1)} %pad_clamp_fusion), kind=kCustom, calls=%fused_computation.1.clone | custom fusion | bytes 2097216 | tf_op jit(solution)/shard_map/jit(_take)/gather | solution.py:37
  40.2 2.0 %convolution_bitcast_fusion.1 = f32[128,16,256]{2,0,1:T(8,128)S(1)} fusion(bf16[16,256,256]{2,1,0:T(8,128)(2,1)S(1)} %copy-done, bf16[16,128,256]{2,1,0:T(8,128)(2,1)} %gather_fusion.2, pred[16]{0:T(512)(128)(4,1)S(1)} %get-tuple-element.32, pred[16]{0:T(512)(128)(4,1)S(1)} %select_bitcast_fusion), kind=kOutput, calls=%fused_computation.15 | convolution fusion | flops 269484032 | bytes 5242912 | tf_op jit(solution)/shard_map/fsb,sab->fsa/dot_general | solution.py:71
  42.3 2.0 %fusion.18 = bf16[128,4,256]{2,1,0:T(4,128)(2,1)S(1)} fusion(f32[128,16,256]{2,0,1:T(8,128)S(1)} %convolution_bitcast_fusion.1, s32[16]{0:T(128)S(1)} %get-tuple-element.31, pred[16]{0:T(512)(128)(4,1)S(1)} %select_bitcast_fusion), kind=kOutput, calls=%fused_computation.19 | convolution fusion | flops 25297024 | bytes 2359376 | tf_op jit(solution)/shard_map/fsa,sr->fra/dot_general | solution.py:73
  44.3 1.6 gather_fusion.3
  45.9 2.4 %bitcast_select_fusion.2 = bf16[128,16,256]{2,0,1:T(8,128)(2,1)} fusion(bf16[16,128,256]{2,1,0:T(8,128)(2,1)} %gather_fusion.3, pred[16]{0:T(512)(128)(4,1)S(1)} %compare_and_fusion.2, pred[16]{0:T(512)(128)(4,1)S(1)} %broadcast_in_dim.99), kind=kLoop, calls=%fused_computation.23 | loop fusion | flops 1048576 | bytes 2097184 | tf_op jit(solution)/shard_map/jit(_where)/select_n | solution.py:38
  48.3 14.4 %all-to-all-done.2 = f32[128,16,256]{2,0,1:T(8,128)} async-done(((f32[128,16,256]{2,0,1:T(8,128)}), f32[128,16,256]{2,0,1:T(8,128)}, u32[]{:S(2)}, u32[]{:S(2)}) %all-to-all-start.2) | async-done | bytes 2097184 | tf_op jit(solution)/shard_map/all_to_all | solution.py:63
  62.6 5.6 %all-to-all-start.1 = ((bf16[128,16,256]{2,0,1:T(8,128)(2,1)}), bf16[128,16,256]{2,0,1:T(8,128)(2,1)}, u32[]{:S(2)}, u32[]{:S(2)}) async-start(bf16[128,16,256]{2,0,1:T(8,128)(2,1)} %bitcast_select_fusion.2), calls=%async_computation.1 | async-start | bytes 2097152 | tf_op jit(solution)/shard_map/all_to_all | solution.py:77
  68.3 0.0 reduce-scatter.2.cloned.1.call-start
  68.3 3.5 %fusion.15 = bf16[128,4,256]{2,1,0:T(4,128)(2,1)S(1)} fusion(f32[128,16,256]{2,0,1:T(8,128)} %all-to-all-done.2, s32[16]{0:T(128)S(1)} %reshape.67, pred[16]{0:T(512)(128)(4,1)S(1)} %broadcast_in_dim.99), kind=kOutput, calls=%fused_computation.18 | convolution fusion | flops 25297024 | bytes 2359376 | tf_op jit(solution)/shard_map/fpb,pr->frb/dot_general | solution.py:68
  71.8 1.6 gather_fusion.5
  73.4 8.9 %all-to-all-done.1 = bf16[128,16,256]{2,0,1:T(8,128)(2,1)} async-done(((bf16[128,16,256]{2,0,1:T(8,128)(2,1)}), bf16[128,16,256]{2,0,1:T(8,128)(2,1)}, u32[]{:S(2)}, u32[]{:S(2)}) %all-to-all-start.1) | async-done | bytes 1048608 | tf_op jit(solution)/shard_map/all_to_all | solution.py:77
  82.3 2.9 %gather_fusion.4 = bf16[16,128,256]{2,1,0:T(8,128)(2,1)} fusion(bf16[128,16,256]{2,0,1:T(8,128)(2,1)} %all-to-all-done.1, s32[1024]{0:T(1024)S(1)} %pad_clamp_fusion), kind=kCustom, calls=%fused_computation.5.clone | custom fusion | bytes 2097216 | tf_op jit(solution)/shard_map/jit(_take)/gather | solution.py:37
  85.2 0.0 copy-start.1
  85.2 0.0 copy-start.2
  85.2 2.5 %fusion.22 = f32[16,256,256]{2,1,0:T(8,128)S(1)} fusion(bf16[16,128,256]{2,1,0:T(8,128)(2,1)} %gather_fusion.4, pred[16]{0:T(512)(128)(4,1)S(1)} %get-tuple-element.32, pred[16]{0:T(512)(128)(4,1)S(1)} %select_bitcast_fusion, bf16[16,128,256]{2,1,0:T(8,128)(2,1)S(1)} %gather_fusion, pred[16]{0:T(512)(128)(4,1)S(1)} %get-tuple-element.30), kind=kOutput, calls=%fused_computation.22 | convolution fusion | flops 270008320 | bytes 6291504 | tf_op jit(solution)/shard_map/fsa,fsb->sab/dot_general | solution.py:80
  87.7 0.0 copy-done.1
  87.7 0.0 copy-done.2
  87.7 3.1 %convolution_add_fusion = f32[16,256,256]{2,1,0:T(8,128)} fusion(f32[16,256,256]{2,1,0:T(8,128)S(1)} %fusion.22, bf16[16,128,256]{2,1,0:T(8,128)(2,1)S(1)} %copy-done.2, pred[16]{0:T(512)(128)(4,1)S(1)} %get-tuple-element.30, bf16[16,128,256]{2,1,0:T(8,128)(2,1)S(1)} %copy-done.1, pred[16]{0:T(512)(128)(4,1)S(1)} %get-tuple-element.32, ...), kind=kOutput, calls=%fused_computation.6 | convolution fusion | flops 271056896 | bytes 10485808 | tf_op jit(solution)/shard_map/fsa,fsb->sab/dot_general | solution.py:81
  90.8 0.0 reduce-scatter.2.cloned.1.call-update
  90.9 77.6 %reduce-scatter.2.cloned.1.call-done = f32[4,256,256]{2,1,0:T(8,128)} async-done(((f32[16,256,256]{2,1,0:T(8,128)}), f32[4,256,256]{2,1,0:T(8,128)}) %reduce-scatter.2.cloned.1.call-update) | async-done | bytes 1048592 | tf_op jit(solution)/shard_map/reduce_scatter | solution.py:84
  (12 shorter events, 0.1 us)
Async XLA Ops:
  6.5 12.1 %copy-start = (bf16[16,256,256]{2,1,0:T(8,128)(2,1)S(1)}, bf16[16,256,256]{2,1,0:T(8,128)(2,1)}, u32[]{:S(2)}) copy-start(bf16[16,256,256]{2,1,0:T(8,128)(2,1)} %param.14) | copy-start | bytes 6291460
  11.8 5.9 %copy-start.3 = (bf16[128,1024]{1,0:T(8,128)(2,1)S(1)}, bf16[128,1024]{1,0:T(8,128)(2,1)}, u32[]{:S(2)}) copy-start(bf16[128,1024]{1,0:T(8,128)(2,1)} %param.13) | copy-start | bytes 786436
  13.0 18.7 %all-to-all-start = ((bf16[128,16,256]{2,0,1:T(8,128)(2,1)}), bf16[128,16,256]{2,0,1:T(8,128)(2,1)}, u32[]{:S(2)}, u32[]{:S(2)}) async-start(bf16[128,16,256]{2,0,1:T(8,128)(2,1)} %bitcast_select_fusion.4), calls=%async_computation | async-start | bytes 2097152 | tf_op jit(solution)/shard_map/all_to_all | solution.py:55
  31.6 31.0 %all-to-all-start.2 = ((f32[128,16,256]{2,0,1:T(8,128)}), f32[128,16,256]{2,0,1:T(8,128)}, u32[]{:S(2)}, u32[]{:S(2)}) async-start(f32[128,16,256]{2,0,1:T(8,128)} %copy.54), calls=%async_computation.2 | async-start | bytes 4194304 | tf_op jit(solution)/shard_map/all_to_all | solution.py:63
  62.6 19.7 %all-to-all-start.1 = ((bf16[128,16,256]{2,0,1:T(8,128)(2,1)}), bf16[128,16,256]{2,0,1:T(8,128)(2,1)}, u32[]{:S(2)}, u32[]{:S(2)}) async-start(bf16[128,16,256]{2,0,1:T(8,128)(2,1)} %bitcast_select_fusion.2), calls=%async_computation.1 | async-start | bytes 2097152 | tf_op jit(solution)/shard_map/all_to_all | solution.py:77
  68.3 100.2 %reduce-scatter.2.cloned.1.call-start = ((), (), s32[]{:S(2)}) async-start(), calls=%async_computation.4 | async-start | bytes 5242880 | tf_op jit(solution)/shard_map/reduce_scatter | solution.py:84
  85.2 2.5 %copy-start.1 = (bf16[16,128,256]{2,1,0:T(8,128)(2,1)S(1)}, bf16[16,128,256]{2,1,0:T(8,128)(2,1)}, u32[]{:S(2)}) copy-start(bf16[16,128,256]{2,1,0:T(8,128)(2,1)} %gather_fusion.2) | copy-start | bytes 3145732
  85.2 2.5 %copy-start.2 = (bf16[16,128,256]{2,1,0:T(8,128)(2,1)S(1)}, bf16[16,128,256]{2,1,0:T(8,128)(2,1)}, u32[]{:S(2)}) copy-start(bf16[16,128,256]{2,1,0:T(8,128)(2,1)} %gather_fusion.5) | copy-start | bytes 3145732
Sparse Core Ops, SparseCore 0:
  91.0 77.4 reduce-scatter.1
where the time goes:
time: 177 us; the launch traced here: 175 us
  waiting for transfers between devices  109 us (62%)
  starting transfers between devices  16 us (9%)
  matrix products  16 us (9%)
  local copies, waits for them, and re-layouts  14.6 us (8%)
  between operations  13.6 us (8%)
  other arithmetic  6.6 us (4%)
    reduce_scatter x1, waiting for transfers between devices, body(): lax.psum_scatter(partial_value, 'depth', scatter_dimension=0, tiled=True)  77.6 us
    all_to_all x1, waiting for transfers between devices, body(): lax.all_to_all(g_outgoing, 'rows', split_axis=1, concat_axis=1, tiled=True)  14.4 us
    all_to_all x1, waiting for transfers between devices, body(): lax.all_to_all(h_outgoing, 'rows', split_axis=1, concat_axis=1, tiled=True)  8.89 us
    gather x4, local copies, waits for them, and re-layouts, pick_tiles(): picked = jnp.take(source, indices, axis=1)  7.87 us
    all_to_all x1, waiting for transfers between devices, body(): lax.all_to_all(outgoing, 'rows', split_axis=1, concat_axis=1, tiled=True)  7.63 us
    all_to_all x1, starting transfers between devices, body(): lax.all_to_all(g_outgoing, 'rows', split_axis=1, concat_axis=1, tiled=True)  5.75 us
    all_to_all x1, starting transfers between devices, body(): lax.all_to_all(h_outgoing, 'rows', split_axis=1, concat_axis=1, tiled=True)  5.65 us
    all_to_all x1, starting transfers between devices, body(): lax.all_to_all(outgoing, 'rows', split_axis=1, concat_axis=1, tiled=True)  4.64 us
  transfers between devices with their start and end apart: 4, of which 4 were waited for; matrix products, arithmetic and copies ran while one was open for 13% of the time, Pallas kernels for 0%

commit v1 on v0

v1 whole, which is shorter than its diff:
```python
import functools

import jax
import jax.numpy as jnp
from jax import lax
from jax.experimental import pallas as pl
from jax.experimental.pallas import tpu as pltpu
from jax.sharding import PartitionSpec as P

MESH = pl.DeviceIdType.MESH
F32 = jnp.float32
BF16 = jnp.bfloat16


def flip(index, mask):
    bit = 1
    out = index
    while bit <= mask:
        if mask & bit:
            out = out + bit * (1 - 2 * ((index // bit) % 2))
        bit *= 2
    return out


def bit_orders(rows):
    bits = []
    bit = 1
    while bit < rows:
        bits.append(bit)
        bit *= 2
    core, chip = bits[:1], bits[1:]
    half = len(chip) // 2
    x_bits, y_bits = chip[:half], chip[half:]
    return (y_bits + x_bits + core, x_bits + y_bits + core)


class Gather:
    def __init__(self, rows, tiles, buf, send_sem, recv_sem, depth_id, me):
        self.rows, self.tiles, self.buf = rows, tiles, buf
        self.send_sem, self.recv_sem = send_sem, recv_sem
        self.depth_id, self.me = depth_id, me
        self.orders = bit_orders(rows)

    def mask(self, half, place):
        out = 0
        for n, bit in enumerate(self.orders[half]):
            if place >> n & 1:
                out |= bit
        return out

    def copy(self, half, place, n):
        mask = self.mask(half, place)
        bit = self.orders[half][n]
        part = self.tiles // 2
        block = flip(self.me, mask)
        ref = self.buf.at[pl.ds(block * self.tiles + half * part, part)]
        sem = half * self.rows + (mask | bit)
        return pltpu.make_async_remote_copy(
            src_ref=ref,
            dst_ref=ref,
            send_sem=self.send_sem.at[sem],
            recv_sem=self.recv_sem.at[sem],
            device_id=(self.depth_id, flip(self.me, bit)),
            device_id_type=MESH,
        )

    def incoming(self, half, place):
        mask = self.mask(half, place)
        part = self.tiles // 2
        ref = self.buf.at[pl.ds(flip(self.me, mask) * self.tiles + half * part, part)]
        sem = half * self.rows + mask
        return pltpu.make_async_remote_copy(
            src_ref=ref,
            dst_ref=ref,
            send_sem=self.send_sem.at[sem],
            recv_sem=self.recv_sem.at[sem],
            device_id=(self.depth_id, flip(self.me, mask)),
            device_id_type=MESH,
        )

    def start(self):
        for n in range(len(self.orders[0])):
            for half in range(2):
                self.copy(half, 0, n).start()

    def forward(self, begin, end):
        count = len(self.orders[0])
        for place in range(begin, end):
            for half in range(2):
                self.incoming(half, place).wait_recv()
                for n in range(place.bit_length(), count):
                    self.copy(half, place, n).start()

    def drain(self):
        count = len(self.orders[0])
        for place in range(self.rows // 2):
            for half in range(2):
                for n in range(place.bit_length(), count):
                    self.copy(half, place, n).wait_send()


def kernel(
    rows,
    depth,
    x_hbm,
    dy_hbm,
    adj_hbm,
    cnt,
    trow,
    tcol,
    out,
    xbuf,
    hbuf,
    adj,
    dyt,
    dy_t,
    g_t,
    terms,
    gout,
    gin,
    gacc,
    send_up,
    send_dn,
    recv_up,
    recv_dn,
    local_sem,
    xs_sem,
    xr_sem,
    hs_sem,
    hr_sem,
    gs_sem,
    gr_sem,
    us_sem,
    ur_sem,
    ds_sem,
    dr_sem,
):
    d = lax.axis_index("depth")
    me = lax.axis_index("rows")
    feat = xbuf.shape[1]
    tile = xbuf.shape[2]
    tiles = dyt.shape[0]
    slots = adj.shape[0]
    share = slots // depth

    local = []
    for j in range(tiles):
        cols = pl.ds(j * tile, tile)
        local.append(
            pltpu.make_async_copy(x_hbm.at[:, cols], xbuf.at[me * tiles + j], local_sem.at[j])
        )
    for j in range(tiles):
        cols = pl.ds(j * tile, tile)
        local.append(
            pltpu.make_async_copy(dy_hbm.at[:, cols], dyt.at[j], local_sem.at[tiles + j])
        )
    local.append(pltpu.make_async_copy(adj_hbm, adj, local_sem.at[2 * tiles]))
    for c in local:
        c.start()

    barrier = pltpu.get_barrier_semaphore()
    for t in range(1, rows):
        pl.semaphore_signal(
            barrier, inc=1, device_id=(d, (me + t) % rows), device_id_type=MESH
        )

    for t in range(1, depth):
        pl.semaphore_signal(
            barrier, inc=1, device_id=((d + t) % depth, me), device_id_type=MESH
        )
    pl.semaphore_wait(barrier, rows - 1 + depth - 1)

    for c in local[:tiles]:
        c.wait()
    xg = Gather(rows, tiles, xbuf, xs_sem, xr_sem, d, me)
    hg = Gather(rows, tiles, hbuf, hs_sem, hr_sem, d, me)
    xg.start()
    for c in local[tiles:]:
        c.wait()

    my_count = cnt[me]

    def g_term(slot, valid):
        row = trow[me, slot]
        g = jnp.dot(dyt[row], adj[slot], preferred_element_type=F32)
        return jnp.where(valid, g, 0.0).astype(BF16)

    def g_body(t, carry):
        o = (me + t) % rows
        first = jnp.int32(0)
        last = jnp.int32(0)
        seen = jnp.int32(0)
        for s in range(slots):
            hit = (s < my_count) & (lax.div(tcol[me, s], jnp.int32(tiles)) == o)
            last = jnp.where(hit, s, last)
            first = jnp.where(hit & (seen == 0), s, first)
            seen = jnp.where(hit, 1, seen)
        gout[t, 0] = g_term(first, seen > 0)
        gout[t, 1] = g_term(last, last > first)
        return carry

    lax.fori_loop(0, rows, g_body, 0)

    for j in range(tiles):
        dy_t[j] = dyt[j].astype(F32).T.astype(BF16)

    def g_copy(t):
        return pltpu.make_async_remote_copy(
            src_ref=gout.at[t],
            dst_ref=gin.at[t],
            send_sem=gs_sem.at[t],
            recv_sem=gr_sem.at[t],
            device_id=(d, (me + t) % rows),
            device_id_type=MESH,
        )

    xg.forward(1, rows // 2)
    for t in range(1, rows):
        g_copy(t).start()
    gin[0] = gout[0]
    xg.forward(rows // 2, rows)

    def h_body(s, carry):
        h = lax.dot_general(
            xbuf[tcol[me, s]], adj[s], (((1,), (1,)), ((), ())), preferred_element_type=F32
        )
        terms[s] = jnp.where(s < my_count, h, 0.0)
        return carry

    lax.fori_loop(0, slots, h_body, 0)

    chunk = min(32, feat)

    def h_sum(c, carry):
        at = pl.ds(pl.multiple_of(c * chunk, chunk), chunk)
        total = [jnp.zeros((chunk, tile), F32) for _ in range(tiles)]
        for s in range(slots):
            term = terms[s, at, :]
            row = trow[me, s]
            for i in range(tiles):
                total[i] = total[i] + jnp.where(row == i, term, 0.0)
        for i in range(tiles):
            hbuf[me * tiles + i, at, :] = total[i].astype(BF16)
        return carry

    lax.fori_loop(0, feat // chunk, h_sum, 0)
    hg.start()

    for t in range(1, rows):
        g_copy(t).wait_recv()
    gacc[...] = jnp.zeros_like(gacc)

    def g_sum(t, carry):
        p = (me + rows - t) % rows
        count = cnt[p]
        seen = jnp.int32(0)
        rank = [jnp.int32(0) for _ in range(tiles)]
        flag = [jnp.int32(0) for _ in range(tiles)]
        for s in range(slots):
            col = tcol[p, s]
            live = s < count
            for j in range(tiles):
                hit = live & (col == me * tiles + j)
                rank[j] = jnp.where(hit, seen, rank[j])
                flag[j] = jnp.where(hit, 1, flag[j])
            seen = jnp.where(live & (lax.div(col, jnp.int32(tiles)) == me), 1, seen)
        for j in range(tiles):
            term = gin[t, rank[j]].astype(F32)
            gacc[j] += jnp.where(flag[j] > 0, term, 0.0)
        return carry

    lax.fori_loop(0, rows, g_sum, 0)
    for j in range(tiles):
        g_t[j] = gacc[j].astype(BF16).astype(F32).T.astype(BF16)

    hg.forward(1, rows)

    def partial(s):
        row = trow[me, s]
        col = tcol[me, s]
        p = jnp.dot(dy_t[row], hbuf[col], preferred_element_type=F32)
        p = p + jnp.dot(g_t[row], xbuf[col], preferred_element_type=F32)
        return jnp.where(s < my_count, p, 0.0)

    def up_copy(s):
        return pltpu.make_async_remote_copy(
            src_ref=send_up.at[s],
            dst_ref=recv_up.at[s],
            send_sem=us_sem.at[s],
            recv_sem=ur_sem.at[s],
            device_id=(lax.rem(d + 1, depth), me),
            device_id_type=MESH,
        )

    def dn_copy(s):
        return pltpu.make_async_remote_copy(
            src_ref=send_dn.at[s],
            dst_ref=recv_dn.at[s],
            send_sem=ds_sem.at[s],
            recv_sem=dr_sem.at[s],
            device_id=(lax.rem(d + depth - 1, depth), me),
            device_id_type=MESH,
        )

    def z_body(n, carry):
        i = n // share
        k = n % share
        t_up = depth - 1 - i
        s_up = t_up * share + k

        @pl.when(t_up > d)
        def _():
            send_up[s_up] = partial(s_up).astype(BF16)

            @pl.when(d > 0)
            def _():
                up_copy(s_up).wait_recv()
                send_up[s_up] = (partial(s_up) + recv_up[s_up].astype(F32)).astype(BF16)

            up_copy(s_up).start()

        t_dn = i
        s_dn = t_dn * share + k

        @pl.when(t_dn < d)
        def _():
            send_dn[s_dn] = partial(s_dn).astype(BF16)

            @pl.when(d < depth - 1)
            def _():
                dn_copy(s_dn).wait_recv()
                send_dn[s_dn] = (partial(s_dn) + recv_dn[s_dn].astype(F32)).astype(BF16)

            dn_copy(s_dn).start()

        return carry

    lax.fori_loop(0, (depth - 1) * share, z_body, 0)

    def own_body(k, carry):
        s = d * share + k
        out[0, k] = partial(s)

        @pl.when(d > 0)
        def _():
            up_copy(s).wait_recv()
            out[0, k] += recv_up[s].astype(F32)

        @pl.when(d < depth - 1)
        def _():
            dn_copy(s).wait_recv()
            out[0, k] += recv_dn[s].astype(F32)

        return carry

    lax.fori_loop(0, share, own_body, 0)

    xg.drain()
    hg.drain()
    for t in range(1, rows):
        g_copy(t).wait_send()

    def z_drain(s, carry):
        t = s // share

        @pl.when(t > d)
        def _():
            up_copy(s).wait_send()

        @pl.when(t < d)
        def _():
            dn_copy(s).wait_send()

        return carry

    lax.fori_loop(0, slots, z_drain, 0)


def body(rows, depth, node_feat, grad_out, adjacency, tile_count, tile_row, tile_col):
    slots, tile = adjacency.shape[:2]
    feat = node_feat.shape[0]
    tiles = node_feat.shape[1] // tile
    share = slots // depth
    dma = pltpu.SemaphoreType.DMA
    any_spec = pl.BlockSpec(memory_space=pl.ANY)
    smem = pl.BlockSpec(memory_space=pltpu.SMEM)
    ntiles = rows * tiles
    return pl.pallas_call(
        functools.partial(kernel, rows, depth),
        out_shape=jax.ShapeDtypeStruct((1, share, tile, tile), F32),
        in_specs=[any_spec] * 3 + [smem] * 3,
        out_specs=pl.BlockSpec(memory_space=pltpu.VMEM),
        scratch_shapes=[
            pltpu.VMEM((ntiles, feat, tile), BF16),
            pltpu.VMEM((ntiles, feat, tile), BF16),
            pltpu.VMEM((slots, tile, tile), BF16),
            pltpu.VMEM((tiles, feat, tile), BF16),
            pltpu.VMEM((tiles, tile, feat), BF16),
            pltpu.VMEM((tiles, tile, feat), BF16),
            pltpu.VMEM((slots, feat, tile), F32),
            pltpu.VMEM((rows, 2, feat, tile), BF16),
            pltpu.VMEM((rows, 2, feat, tile), BF16),
            pltpu.VMEM((tiles, feat, tile), F32),
            pltpu.VMEM((slots, tile, tile), BF16),
            pltpu.VMEM((slots, tile, tile), BF16),
            pltpu.VMEM((slots, tile, tile), BF16),
            pltpu.VMEM((slots, tile, tile), BF16),
            dma((2 * tiles + 1,)),
            dma((2 * rows,)),
            dma((2 * rows,)),
            dma((2 * rows,)),
            dma((2 * rows,)),
            dma((rows,)),
            dma((rows,)),
            dma((slots,)),
            dma((slots,)),
            dma((slots,)),
            dma((slots,)),
        ],
        compiler_params=pltpu.CompilerParams(
            collective_id=0, has_side_effects=True, vmem_limit_bytes=44 * 1024 * 1024
        ),
    )(node_feat, grad_out, adjacency, tile_count, tile_row, tile_col)


def solution(mesh):
    in_specs = (P("depth", "rows"), P("depth", "rows"), P("rows", None, None), P(), P(), P())
    out_specs = P("rows", "depth", None, None)
    call = functools.partial(body, mesh.shape["rows"], mesh.shape["depth"])
    return jax.shard_map(call, mesh=mesh, in_specs=in_specs, out_specs=out_specs, check_vma=False)
```

time: 177 us -> 97.7 us (0.55)
  waiting for transfers between devices: 109 us -> 0 us
  Pallas kernels: 0 us -> 89.6 us
  matrix products: 16 us -> 0 us
  starting transfers between devices: 16 us -> 0 us
  between operations: 13.6 us -> 0.02 us
  local copies, waits for them, and re-layouts: 14.6 us -> 6.49 us
  other arithmetic: 6.6 us -> 0 us
    pallas_call x0 -> x1, Pallas kernels: none -> 89.6 us  [body(): pl.pallas_call(functools.partial(kernel, rows, depth), out_shape=jax.Shap...]
    reduce_scatter x1 -> x0, waiting for transfers between devices: 77.6 us -> none  [body(): lax.psum_scatter(partial_value, 'depth', scatter_dimension=0, tiled=True)]
    all_to_all x3 -> x0, waiting for transfers between devices: 30.9 us -> none  [the longest x1 14.4 us: body(): lax.all_to_all(g_outgoing, 'rows', split_axis=1, concat_axis=1, tiled=True)]
    all_to_all x3 -> x0, starting transfers between devices: 16 us -> none  [the longest x1 5.75 us: body(): lax.all_to_all(g_outgoing, 'rows', split_axis=1, concat_axis=1, tiled=True)]
    dot_general x7 -> x0, matrix products: 16 us -> none  [the longest x1 3.49 us: body(): jnp.einsum('fpb,pr->frb', g_incoming, col_onehot, precision=top_precision)]
    gather x6 -> x0, local copies, waits for them, and re-layouts: 10.1 us -> none  [the longest x4 7.87 us: pick_tiles(): picked = jnp.take(source, indices, axis=1)]
    unnamed x10 -> x13, local copies, waits for them, and re-layouts: 1.31 us -> 6.49 us
    select_n x6 -> x0, other arithmetic: 4.47 us -> none  [the longest x2 3.61 us: pick_tiles(): return jnp.where(keep[None, :, None], picked, jnp.zeros((), source.dtype))]
  transfers between devices with their start and end apart: 4 -> 0, of which waited for: 4 -> 0; matrix products, arithmetic and copies ran while one was open for 13% -> 0% of each run, Pallas kernels for 0% -> 0%
where the time goes in v1:
time: 97.7 us; the launch traced here: 96.1 us
  Pallas kernels  89.6 us (92%)
  local copies, waits for them, and re-layouts  6.49 us (7%)
    pallas_call x1, Pallas kernels, body(): pl.pallas_call(functools.partial(kernel, rows, depth), out_shape=jax.Shap...  89.6 us
    unnamed x13, local copies, waits for them, and re-layouts  6.49 us

profile of v1, /device:TPU:18, one launch (start us, length us, event | category | flops | bytes accessed | tf_op | source)
XLA Modules:
  0.0 96.1 jit_solution(15370296802847523038)
XLA Ops:
  0.0 0.0 copy-start
  0.0 1.6 %copy-done = bf16[16,256,256]{2,1,0:T(8,128)(2,1)S(1)} copy-done((bf16[16,256,256]{2,1,0:T(8,128)(2,1)S(1)}, bf16[16,256,256]{2,1,0:T(8,128)(2,1)}, u32[]{:S(2)}) %copy-start) | copy-done | bytes 2097176
  1.6 0.0 copy-start.1
  1.6 0.9 copy-done.1
  2.5 0.0 copy-start.2
  2.5 0.9 copy-done.2
  3.5 0.0 copy-start.3
  3.5 0.7 copy-done.3
  4.2 0.0 copy-start.4
  4.2 0.7 copy-done.4
  4.9 0.0 copy-start.5
  4.9 0.7 copy-done.5
  5.5 89.6 %shard_map.64 = f32[1,4,256,256]{3,2,1,0:T(8,128)S(1)} custom-call(bf16[128,1024]{1,0:T(8,128)(2,1)S(1)} %copy-done.1, bf16[128,1024]{1,0:T(8,128)(2,1)S(1)} %copy-done.2, bf16[16,256,256]{2,1,0:T(8,128)(2,1)S(1)} %copy-done, s32[8]{0:T(128)S(1)} %copy-done.5, s32[8,16]{1,0:T(8,128)S(1)} %copy-done.3, s32[8,16]{1,0:T(8,128)S(1)} %copy-done.4), custom_call_target="tpu_custom_call" | custom-call | tf_op jit(solution)/shard_map/pallas_call | solution.py:388
  95.1 1.0 %copy.8 = f32[1,4,256,256]{3,2,1,0:T(8,128)} copy(f32[1,4,256,256]{3,2,1,0:T(8,128)S(1)} %shard_map.64) | data formatting | bytes 2097152
Async XLA Ops:
  0.0 1.6 %copy-start = (bf16[16,256,256]{2,1,0:T(8,128)(2,1)S(1)}, bf16[16,256,256]{2,1,0:T(8,128)(2,1)}, u32[]{:S(2)}) copy-start(bf16[16,256,256]{2,1,0:T(8,128)(2,1)} %adj_hbm.1) | copy-start | bytes 6291460
  1.6 0.9 copy-start.1
  2.5 0.9 copy-start.2
  3.5 0.7 copy-start.3
  4.2 0.7 copy-start.4
  4.9 0.7 copy-start.5

commit v2 on v1

v2 whole, which is shorter than its diff:
```python
import functools

import jax
import jax.numpy as jnp
from jax import lax
from jax.experimental import pallas as pl
from jax.experimental.pallas import tpu as pltpu
from jax.sharding import PartitionSpec as P

MESH = pl.DeviceIdType.MESH
F32 = jnp.float32
BF16 = jnp.bfloat16


def flip(index, mask):
    bit = 1
    out = index
    while bit <= mask:
        if mask & bit:
            out = out + bit * (1 - 2 * ((index // bit) % 2))
        bit *= 2
    return out


def bit_orders(rows):
    bits = []
    bit = 1
    while bit < rows:
        bits.append(bit)
        bit *= 2
    core, chip = bits[:1], bits[1:]
    half = len(chip) // 2
    x_bits, y_bits = chip[:half], chip[half:]
    return (y_bits + x_bits + core, x_bits + y_bits + core)


class Gather:
    def __init__(self, rows, tiles, buf, send_sem, recv_sem, depth_id, me):
        self.rows, self.tiles, self.buf = rows, tiles, buf
        self.send_sem, self.recv_sem = send_sem, recv_sem
        self.depth_id, self.me = depth_id, me
        self.orders = bit_orders(rows)

    def mask(self, half, place):
        out = 0
        for n, bit in enumerate(self.orders[half]):
            if place >> n & 1:
                out |= bit
        return out

    def copy(self, half, place, n):
        mask = self.mask(half, place)
        bit = self.orders[half][n]
        part = self.tiles // 2
        block = flip(self.me, mask)
        ref = self.buf.at[pl.ds(block * self.tiles + half * part, part)]
        sem = half * self.rows + (mask | bit)
        return pltpu.make_async_remote_copy(
            src_ref=ref,
            dst_ref=ref,
            send_sem=self.send_sem.at[sem],
            recv_sem=self.recv_sem.at[sem],
            device_id=(self.depth_id, flip(self.me, bit)),
            device_id_type=MESH,
        )

    def incoming(self, half, place):
        mask = self.mask(half, place)
        part = self.tiles // 2
        ref = self.buf.at[pl.ds(flip(self.me, mask) * self.tiles + half * part, part)]
        sem = half * self.rows + mask
        return pltpu.make_async_remote_copy(
            src_ref=ref,
            dst_ref=ref,
            send_sem=self.send_sem.at[sem],
            recv_sem=self.recv_sem.at[sem],
            device_id=(self.depth_id, flip(self.me, mask)),
            device_id_type=MESH,
        )

    def start(self):
        for n in range(len(self.orders[0])):
            for half in range(2):
                self.copy(half, 0, n).start()

    def forward(self, begin, end):
        count = len(self.orders[0])
        for place in range(begin, end):
            for half in range(2):
                self.incoming(half, place).wait_recv()
                for n in range(place.bit_length(), count):
                    self.copy(half, place, n).start()

    def drain(self):
        count = len(self.orders[0])
        for place in range(self.rows // 2):
            for half in range(2):
                for n in range(place.bit_length(), count):
                    self.copy(half, place, n).wait_send()


def kernel(
    rows,
    depth,
    x_hbm,
    dy_hbm,
    adj_hbm,
    cnt_hbm,
    trow_hbm,
    tcol_hbm,
    out,
    cnt,
    trow,
    tcol,
    gtab,
    xbuf,
    hbuf,
    adj,
    dyt,
    dy_t,
    g_t,
    dy_t2,
    g_t2,
    xpick,
    hpick,
    x2,
    h2,
    terms,
    gterm,
    gout,
    gin,
    gacc,
    send_up,
    send_dn,
    recv_up,
    recv_dn,
    local_sem,
    xs_sem,
    xr_sem,
    hs_sem,
    hr_sem,
    gs_sem,
    gr_sem,
    us_sem,
    ur_sem,
    ds_sem,
    dr_sem,
    feat_ssem,
    feat_rsem,
    h2s_sem,
    h2r_sem,
):
    d = lax.axis_index("depth")
    me = lax.axis_index("rows")
    feat = xbuf.shape[1]
    tile = xbuf.shape[2]
    tiles = dyt.shape[0]
    slots = adj.shape[0]
    share = slots // depth
    last_d = depth - 1
    group = 4

    x_local, dy_local = [], []
    for j in range(tiles):
        cols = pl.ds(j * tile, tile)
        x_local.append(
            pltpu.make_async_copy(x_hbm.at[:, cols], xbuf.at[me * tiles + j], local_sem.at[j])
        )
        dy_local.append(
            pltpu.make_async_copy(dy_hbm.at[:, cols], dyt.at[j], local_sem.at[tiles + j])
        )
    adj_local = pltpu.make_async_copy(adj_hbm, adj, local_sem.at[2 * tiles])
    table_local = [
        pltpu.make_async_copy(src, dst, local_sem.at[2 * tiles + 1 + n])
        for n, (src, dst) in enumerate(((cnt_hbm, cnt), (trow_hbm, trow), (tcol_hbm, tcol)))
    ]
    for c in x_local + table_local + dy_local + [adj_local]:
        c.start()

    barrier = pltpu.get_barrier_semaphore()
    for t in range(1, rows):
        pl.semaphore_signal(
            barrier, inc=1, device_id=(d, (me + t) % rows), device_id_type=MESH
        )
    for t in range(1, depth):
        pl.semaphore_signal(
            barrier, inc=1, device_id=((d + t) % depth, me), device_id_type=MESH
        )

    @pl.when(d <= 1)
    def _():
        recv_up[...] = jnp.zeros_like(recv_up)

    @pl.when(d >= last_d - 1)
    def _():
        recv_dn[...] = jnp.zeros_like(recv_dn)

    for t in range(rows):
        gin[t, 2] = jnp.zeros((feat, tile), BF16)
    gacc[...] = jnp.zeros_like(gacc)

    pl.semaphore_wait(barrier, rows - 1 + depth - 1)

    for c in x_local:
        c.wait()
    xg = Gather(rows, tiles, xbuf, xs_sem, xr_sem, d, me)
    hg = Gather(rows, tiles, hbuf, hs_sem, hr_sem, d, me)
    xg.start()
    for c in table_local + dy_local + [adj_local]:
        c.wait()

    my_count = cnt[me]

    def g_body(n, carry):
        for u in range(group):
            s = n * group + u
            g = jnp.dot(dyt[trow[me, s]], adj[s], preferred_element_type=F32)
            gterm[s] = g.astype(BF16)
        return carry

    lax.fori_loop(0, slots // group, g_body, 0)

    def g_pick(t, carry):
        o = (me + t) % rows
        first = jnp.int32(0)
        last = jnp.int32(0)
        seen = jnp.int32(0)
        for s in range(slots):
            hit = (s < my_count) & (lax.div(tcol[me, s], jnp.int32(tiles)) == o)
            last = jnp.where(hit, s, last)
            first = jnp.where(hit & (seen == 0), s, first)
            seen = jnp.where(hit, 1, seen)
        gout[t, 0] = gterm[first]
        gout[t, 1] = gterm[last]
        return carry

    lax.fori_loop(0, rows, g_pick, 0)

    def g_copy(t):
        return pltpu.make_async_remote_copy(
            src_ref=gout.at[t],
            dst_ref=gin.at[t, pl.ds(0, 2)],
            send_sem=gs_sem.at[t],
            recv_sem=gr_sem.at[t],
            device_id=(d, (me + t) % rows),
            device_id_type=MESH,
        )

    xg.forward(1, rows // 4)
    for t in range(1, rows):
        g_copy(t).start()
    gin[0, pl.ds(0, 2)] = gout[0]

    is_end = (d == 0) | (d == last_d)
    is_next = (d == 1) | (d == last_d - 1)
    inner = jnp.where(d < 2, 1 - d, 2 * last_d - 1 - d)
    inner = jnp.where(d < 2, inner, jnp.where(d >= last_d - 1, inner, 0))
    end_id = (inner, me)
    kept = (depth - 1) * share
    low = jnp.where(d < 2, share, 0)

    def feat_copy(src, dst, n):
        return pltpu.make_async_remote_copy(
            src_ref=src,
            dst_ref=dst,
            send_sem=feat_ssem.at[n],
            recv_sem=feat_rsem.at[n],
            device_id=end_id,
            device_id_type=MESH,
        )

    def dy_feat():
        return feat_copy(dy_t, dy_t2, 0)

    def x_feat():
        at = pl.ds(low, kept)
        return feat_copy(xpick.at[at], x2.at[at], 1)

    def g_feat():
        return feat_copy(g_t, g_t2, 2)

    def h_feat(s):
        return pltpu.make_async_remote_copy(
            src_ref=hpick.at[s],
            dst_ref=h2.at[s],
            send_sem=h2s_sem.at[s],
            recv_sem=h2r_sem.at[s],
            device_id=end_id,
            device_id_type=MESH,
        )

    for j in range(tiles):
        dy_t[j] = dyt[j].astype(F32).T.astype(BF16)

    @pl.when(is_end)
    def _():
        dy_feat().start()

    def g_table(t, carry):
        p = (me + rows - t) % rows
        count = cnt[p]
        seen = jnp.int32(0)
        rank = [jnp.int32(2) for _ in range(tiles)]
        for s in range(slots):
            off = tcol[p, s] - me * tiles
            off = jnp.where(s < count, off, -1)
            for j in range(tiles):
                rank[j] = jnp.where(off == j, seen, rank[j])
            seen = jnp.where((off >= 0) & (off < tiles), 1, seen)
        for j in range(tiles):
            gtab[t * tiles + j] = rank[j]
        return carry

    lax.fori_loop(0, rows, g_table, 0)

    xg.forward(rows // 4, rows)

    def h_body(n, carry):
        for u in range(group):
            s = n * group + u
            x = xbuf[tcol[me, s]]
            xpick[s] = x
            terms[s] = lax.dot_general(
                x, adj[s], (((1,), (1,)), ((), ())), preferred_element_type=F32
            )
        return carry

    lax.fori_loop(0, slots // group, h_body, 0)

    chunk = min(32, feat)

    def h_sum(c, carry):
        at = pl.ds(pl.multiple_of(c * chunk, chunk), chunk)
        total = [jnp.zeros((chunk, tile), F32) for _ in range(tiles)]
        for s in range(slots):
            term = terms[s, at, :]
            row = jnp.where(s < my_count, trow[me, s], -1)
            for i in range(tiles):
                total[i] = total[i] + jnp.where(row == i, term, 0.0)
        for i in range(tiles):
            hbuf[me * tiles + i, at, :] = total[i].astype(BF16)
        return carry

    lax.fori_loop(0, feat // chunk, h_sum, 0)
    hg.start()

    @pl.when(is_end)
    def _():
        x_feat().start()

    for t in range(1, rows):
        g_copy(t).wait_recv()

    def g_sum(t, carry):
        for j in range(tiles):
            gacc[j] += gin[t, gtab[t * tiles + j]].astype(F32)
        return carry

    lax.fori_loop(0, rows, g_sum, 0)
    for j in range(tiles):
        g_t[j] = gacc[j].astype(BF16).astype(F32).T.astype(BF16)

    @pl.when(is_end)
    def _():
        g_feat().start()

    hg.forward(1, rows)

    def up_slot(n):
        return (last_d - n // share) * share + n % share

    def h_send(n, carry):
        s = jnp.where(d == 0, up_slot(n), n)
        hpick[s] = hbuf[tcol[me, s]]
        h_feat(s).start()
        return carry

    @pl.when(is_end)
    def _():
        lax.fori_loop(0, kept, h_send, 0)

    @pl.when(is_next)
    def _():
        dy_feat().wait_recv()
        x_feat().wait_recv()
        g_feat().wait_recv()

    def dots(dy, g, h, x):
        lhs = jnp.concatenate([dy, g], axis=1)
        rhs = jnp.concatenate([h, x], axis=0)
        return jnp.dot(lhs, rhs, preferred_element_type=F32)

    def live(s, p):
        return jnp.where(s < my_count, p, 0.0)

    def partial(s):
        row = trow[me, s]
        col = tcol[me, s]
        return live(s, dots(dy_t[row], g_t[row], hbuf[col], xbuf[col]))

    def partial_end(s):
        row = trow[me, s]
        return live(s, dots(dy_t2[row], g_t2[row], h2[s], x2[s]))

    def up_copy(s):
        return pltpu.make_async_remote_copy(
            src_ref=send_up.at[s],
            dst_ref=recv_up.at[s],
            send_sem=us_sem.at[s],
            recv_sem=ur_sem.at[s],
            device_id=((d + 1) % depth, me),
            device_id_type=MESH,
        )

    def dn_copy(s):
        return pltpu.make_async_remote_copy(
            src_ref=send_dn.at[s],
            dst_ref=recv_dn.at[s],
            send_sem=ds_sem.at[s],
            recv_sem=dr_sem.at[s],
            device_id=((d + depth - 1) % depth, me),
            device_id_type=MESH,
        )

    def up_step(n):
        s = up_slot(n)

        @pl.when((d == 1) & (n < (last_d - 1) * share))
        def _():
            p = partial(s)
            h_feat(s).wait_recv()
            send_up[s] = (p + partial_end(s)).astype(BF16)
            up_copy(s).start()

        @pl.when((d > 1) & (d < last_d) & (n < (last_d - d) * share))
        def _():
            p = partial(s)
            up_copy(s).wait_recv()
            send_up[s] = (p + recv_up[s].astype(F32)).astype(BF16)
            up_copy(s).start()

    def dn_step(n):
        @pl.when((d == last_d - 1) & (n < d * share))
        def _():
            p = partial(n)
            h_feat(n).wait_recv()
            send_dn[n] = (p + partial_end(n)).astype(BF16)
            dn_copy(n).start()

        @pl.when((d > 0) & (d < last_d - 1) & (n < d * share))
        def _():
            p = partial(n)
            dn_copy(n).wait_recv()
            send_dn[n] = (p + recv_dn[n].astype(F32)).astype(BF16)
            dn_copy(n).start()

    lag = 1

    def z_body(n, carry):
        @pl.when(d < last_d - 1)
        def _():
            up_step(n)

            @pl.when(n >= lag)
            def _():
                dn_step(n - lag)

        @pl.when(d == last_d - 1)
        def _():
            dn_step(n)

            @pl.when(n >= lag)
            def _():
                up_step(n - lag)

        return carry

    @pl.when((d > 0) & (d < last_d))
    def _():
        lax.fori_loop(0, (last_d - 1) * share + lag, z_body, 0)

    def own_first(k, carry):
        out[0, k] = partial(d * share + k)
        return carry

    lax.fori_loop(0, share, own_first, 0)

    def own_end(k, carry):
        s = d * share + k
        h_feat(s).wait_recv()
        out[0, k] += partial_end(s)
        return carry

    @pl.when(is_next)
    def _():
        lax.fori_loop(0, share, own_end, 0)

    def own_up(k, carry):
        s = d * share + k
        up_copy(s).wait_recv()
        out[0, k] += recv_up[s].astype(F32)
        return carry

    def own_dn(k, carry):
        s = d * share + k
        dn_copy(s).wait_recv()
        out[0, k] += recv_dn[s].astype(F32)
        return carry

    @pl.when(d >= 2)
    def _():
        lax.fori_loop(0, share, own_up, 0)

    @pl.when(d <= last_d - 2)
    def _():
        lax.fori_loop(0, share, own_dn, 0)

    xg.drain()
    hg.drain()
    for t in range(1, rows):
        g_copy(t).wait_send()

    @pl.when(is_end)
    def _():
        dy_feat().wait_send()
        x_feat().wait_send()
        g_feat().wait_send()

        def h_drain(n, carry):
            h_feat(low + n).wait_send()
            return carry

        lax.fori_loop(0, kept, h_drain, 0)

    def z_drain(s, carry):
        t = s // share

        @pl.when((d > 0) & (d < last_d) & (t > d))
        def _():
            up_copy(s).wait_send()

        @pl.when((d > 0) & (d < last_d) & (t < d))
        def _():
            dn_copy(s).wait_send()

        return carry

    lax.fori_loop(0, slots, z_drain, 0)


def body(rows, depth, node_feat, grad_out, adjacency, tile_count, tile_row, tile_col):
    slots, tile = adjacency.shape[:2]
    feat = node_feat.shape[0]
    tiles = node_feat.shape[1] // tile
    share = slots // depth
    dma = pltpu.SemaphoreType.DMA
    hbm = pl.BlockSpec(memory_space=pltpu.HBM)
    ntiles = rows * tiles
    node = pltpu.VMEM((ntiles, feat, tile), BF16)
    turned = pltpu.VMEM((tiles, tile, feat), BF16)
    picked = pltpu.VMEM((slots, feat, tile), BF16)
    sums = pltpu.VMEM((slots, tile, tile), BF16)
    return pl.pallas_call(
        functools.partial(kernel, rows, depth),
        out_shape=jax.ShapeDtypeStruct((1, share, tile, tile), F32),
        in_specs=[hbm] * 6,
        out_specs=pl.BlockSpec(memory_space=pltpu.VMEM),
        scratch_shapes=[
            pltpu.SMEM(tile_count.shape, jnp.int32),
            pltpu.SMEM(tile_row.shape, jnp.int32),
            pltpu.SMEM(tile_col.shape, jnp.int32),
            pltpu.SMEM((rows * tiles,), jnp.int32),
            node,
            node,
            sums,
            pltpu.VMEM((tiles, feat, tile), BF16),
            turned,
            turned,
            turned,
            turned,
            picked,
            picked,
            picked,
            picked,
            pltpu.VMEM((slots, feat, tile), F32),
            picked,
            pltpu.VMEM((rows, 2, feat, tile), BF16),
            pltpu.VMEM((rows, 3, feat, tile), BF16),
            pltpu.VMEM((tiles, feat, tile), F32),
            sums,
            sums,
            sums,
            sums,
            dma((2 * tiles + 4,)),
            dma((2 * rows,)),
            dma((2 * rows,)),
            dma((2 * rows,)),
            dma((2 * rows,)),
            dma((rows,)),
            dma((rows,)),
            dma((slots,)),
            dma((slots,)),
            dma((slots,)),
            dma((slots,)),
            dma((3,)),
            dma((3,)),
            dma((slots,)),
            dma((slots,)),
        ],
        compiler_params=pltpu.CompilerParams(
            collective_id=0, has_side_effects=True, vmem_limit_bytes=48 * 1024 * 1024
        ),
    )(node_feat, grad_out, adjacency, tile_count, tile_row, tile_col)


def solution(mesh):
    in_specs = (P("depth", "rows"), P("depth", "rows"), P("rows", None, None), P(), P(), P())
    out_specs = P("rows", "depth", None, None)
    call = functools.partial(body, mesh.shape["rows"], mesh.shape["depth"])
    return jax.shard_map(call, mesh=mesh, in_specs=in_specs, out_specs=out_specs, check_vma=False)
```

time: 97.7 us -> 82.1 us (0.84)
  the two profiles are of different devices: /device:TPU:18 before, /device:TPU:9 now
where the time goes in v2:
time: 82.1 us; the launch traced here: 81.9 us
  Pallas kernels  75.4 us (92%)
  local copies, waits for them, and re-layouts  6.49 us (8%)
    pallas_call x1, Pallas kernels, body(): pl.pallas_call(functools.partial(kernel, rows, depth), out_shape=jax.Shap...  75.4 us
    unnamed x13, local copies, waits for them, and re-layouts  6.49 us

profile of v2, /device:TPU:9, one launch (start us, length us, event | category | flops | bytes accessed | tf_op | source)
XLA Modules:
  0.0 81.9 jit_solution(681742453134088086)
XLA Ops:
  0.0 0.0 copy-start
  0.0 1.6 %copy-done = bf16[16,256,256]{2,1,0:T(8,128)(2,1)S(1)} copy-done((bf16[16,256,256]{2,1,0:T(8,128)(2,1)S(1)}, bf16[16,256,256]{2,1,0:T(8,128)(2,1)}, u32[]{:S(2)}) %copy-start) | copy-done | bytes 2097176
  1.6 0.0 copy-start.1
  1.6 0.9 %copy-done.1 = bf16[128,1024]{1,0:T(8,128)(2,1)S(1)} copy-done((bf16[128,1024]{1,0:T(8,128)(2,1)S(1)}, bf16[128,1024]{1,0:T(8,128)(2,1)}, u32[]{:S(2)}) %copy-start.1) | copy-done | bytes 262168
  2.5 0.0 copy-start.2
  2.5 0.9 %copy-done.2 = bf16[128,1024]{1,0:T(8,128)(2,1)S(1)} copy-done((bf16[128,1024]{1,0:T(8,128)(2,1)S(1)}, bf16[128,1024]{1,0:T(8,128)(2,1)}, u32[]{:S(2)}) %copy-start.2) | copy-done | bytes 262168
  3.5 0.0 copy-start.3
  3.5 0.7 copy-done.3
  4.2 0.0 copy-start.4
  4.2 0.7 copy-done.4
  4.9 0.0 copy-start.5
  4.9 0.7 copy-done.5
  5.5 75.4 %shard_map.64 = f32[1,4,256,256]{3,2,1,0:T(8,128)S(1)} custom-call(bf16[128,1024]{1,0:T(8,128)(2,1)S(1)} %copy-done.1, bf16[128,1024]{1,0:T(8,128)(2,1)S(1)} %copy-done.2, bf16[16,256,256]{2,1,0:T(8,128)(2,1)S(1)} %copy-done, s32[8]{0:T(128)S(1)} %copy-done.5, s32[8,16]{1,0:T(8,128)S(1)} %copy-done.3, s32[8,16]{1,0:T(8,128)S(1)} %copy-done.4), custom_call_target="tpu_custom_call" | custom-call | tf_op jit(solution)/shard_map/pallas_call | solution.py:563
  80.9 1.0 %copy.8 = f32[1,4,256,256]{3,2,1,0:T(8,128)} copy(f32[1,4,256,256]{3,2,1,0:T(8,128)S(1)} %shard_map.64) | data formatting | bytes 2097152
Async XLA Ops:
  0.0 1.6 %copy-start = (bf16[16,256,256]{2,1,0:T(8,128)(2,1)S(1)}, bf16[16,256,256]{2,1,0:T(8,128)(2,1)}, u32[]{:S(2)}) copy-start(bf16[16,256,256]{2,1,0:T(8,128)(2,1)} %adj_hbm.1) | copy-start | bytes 6291460
  1.6 0.9 %copy-start.1 = (bf16[128,1024]{1,0:T(8,128)(2,1)S(1)}, bf16[128,1024]{1,0:T(8,128)(2,1)}, u32[]{:S(2)}) copy-start(bf16[128,1024]{1,0:T(8,128)(2,1)} %x_hbm.1) | copy-start | bytes 786436
  2.5 0.9 %copy-start.2 = (bf16[128,1024]{1,0:T(8,128)(2,1)S(1)}, bf16[128,1024]{1,0:T(8,128)(2,1)}, u32[]{:S(2)}) copy-start(bf16[128,1024]{1,0:T(8,128)(2,1)} %dy_hbm.1) | copy-start | bytes 786436
  3.5 0.7 copy-start.3
  4.2 0.7 copy-start.4
  4.9 0.7 copy-start.5

commit v3 on v2

--- a/solution.py
+++ b/solution.py
@@ -32,6 +32,13 @@
     half = len(chip) // 2
     x_bits, y_bits = chip[:half], chip[half:]
     return (y_bits + x_bits + core, x_bits + y_bits + core)
+
+
+def peer(index, mask, bits):
+    out = index
+    for bit in bits:
+        out = out + bit * (1 - 2 * ((index // bit) % 2)) * ((mask // bit) % 2)
+    return out
 
 
 class Gather:
@@ -108,6 +115,7 @@
     cnt_hbm,
     trow_hbm,
     tcol_hbm,
+    out_hbm,
     out,
     cnt,
     trow,
@@ -159,6 +167,7 @@
     share = slots // depth
     last_d = depth - 1
     group = 4
+    bits = sorted(bit_orders(rows)[0])
 
     x_local, dy_local = [], []
     for j in range(tiles):
@@ -221,7 +230,7 @@
     lax.fori_loop(0, slots // group, g_body, 0)
 
     def g_pick(t, carry):
-        o = (me + t) % rows
+        o = peer(me, t, bits)
         first = jnp.int32(0)
         last = jnp.int32(0)
         seen = jnp.int32(0)
@@ -242,12 +251,13 @@
             dst_ref=gin.at[t, pl.ds(0, 2)],
             send_sem=gs_sem.at[t],
             recv_sem=gr_sem.at[t],
-            device_id=(d, (me + t) % rows),
+            device_id=(d, flip(me, t)),
             device_id_type=MESH,
         )
 
     xg.forward(1, rows // 4)
-    for t in range(1, rows):
+    order = sorted(range(1, rows), key=lambda t: (-bin(t // 2).count("1"), t % 2, t))
+    for t in order:
         g_copy(t).start()
     gin[0, pl.ds(0, 2)] = gout[0]
 
@@ -297,7 +307,7 @@
         dy_feat().start()
 
     def g_table(t, carry):
-        p = (me + rows - t) % rows
+        p = peer(me, t, bits)
         count = cnt[p]
         seen = jnp.int32(0)
         rank = [jnp.int32(2) for _ in range(tiles)]
@@ -348,6 +358,7 @@
     def _():
         x_feat().start()
 
+    hg.forward(1, rows // 4)
     for t in range(1, rows):
         g_copy(t).wait_recv()
 
@@ -364,7 +375,7 @@
     def _():
         g_feat().start()
 
-    hg.forward(1, rows)
+    hg.forward(rows // 4, rows)
 
     def up_slot(n):
         return (last_d - n // share) * share + n % share
@@ -480,7 +491,7 @@
         lax.fori_loop(0, (last_d - 1) * share + lag, z_body, 0)
 
     def own_first(k, carry):
-        out[0, k] = partial(d * share + k)
+        out[k] = partial(d * share + k)
         return carry
 
     lax.fori_loop(0, share, own_first, 0)
@@ -488,7 +499,7 @@
     def own_end(k, carry):
         s = d * share + k
         h_feat(s).wait_recv()
-        out[0, k] += partial_end(s)
+        out[k] += partial_end(s)
         return carry
 
     @pl.when(is_next)
@@ -498,13 +509,13 @@
     def own_up(k, carry):
         s = d * share + k
         up_copy(s).wait_recv()
-        out[0, k] += recv_up[s].astype(F32)
+        out[k] += recv_up[s].astype(F32)
         return carry
 
     def own_dn(k, carry):
         s = d * share + k
         dn_copy(s).wait_recv()
-        out[0, k] += recv_dn[s].astype(F32)
+        out[k] += recv_dn[s].astype(F32)
         return carry
 
     @pl.when(d >= 2)
@@ -515,6 +526,8 @@
     def _():
         lax.fori_loop(0, share, own_dn, 0)
 
+    result = pltpu.make_async_copy(out, out_hbm.at[0], local_sem.at[2 * tiles + 4])
+    result.start()
     xg.drain()
     hg.drain()
     for t in range(1, rows):
@@ -546,6 +559,7 @@
         return carry
 
     lax.fori_loop(0, slots, z_drain, 0)
+    result.wait()
 
 
 def body(rows, depth, node_feat, grad_out, adjacency, tile_count, tile_row, tile_col):
@@ -564,8 +578,9 @@
         functools.partial(kernel, rows, depth),
         out_shape=jax.ShapeDtypeStruct((1, share, tile, tile), F32),
         in_specs=[hbm] * 6,
-        out_specs=pl.BlockSpec(memory_space=pltpu.VMEM),
+        out_specs=hbm,
         scratch_shapes=[
+            pltpu.VMEM((share, tile, tile), F32),
             pltpu.SMEM(tile_count.shape, jnp.int32),
             pltpu.SMEM(tile_row.shape, jnp.int32),
             pltpu.SMEM(tile_col.shape, jnp.int32),
@@ -591,7 +606,7 @@
             sums,
             sums,
             sums,
-            dma((2 * tiles + 4,)),
+            dma((2 * tiles + 5,)),
             dma((2 * rows,)),
             dma((2 * rows,)),
             dma((2 * rows,)),
@@ -608,7 +623,7 @@
             dma((slots,)),
         ],
         compiler_params=pltpu.CompilerParams(
-            collective_id=0, has_side_effects=True, vmem_limit_bytes=48 * 1024 * 1024
+            collective_id=0, has_side_effects=True, vmem_limit_bytes=64 * 1024 * 1024
         ),
     )(node_feat, grad_out, adjacency, tile_count, tile_row, tile_col)
 

time: 82.1 us -> 78.2 us (0.952)
  the two profiles are of different devices: /device:TPU:9 before, /device:TPU:18 now
where the time goes in v3:
time: 78.2 us; the launch traced here: 77.1 us
  Pallas kernels  74.8 us (96%)
  local copies, waits for them, and re-layouts  2.29 us (3%)
    pallas_call x1, Pallas kernels, body(): pl.pallas_call(functools.partial(kernel, rows, depth), out_shape=jax.Shap...  74.8 us
    unnamed x1, local copies, waits for them, and re-layouts  2.29 us

profile of v3, /device:TPU:18, one launch (start us, length us, event | category | flops | bytes accessed | tf_op | source)
XLA Modules:
  0.0 77.1 jit_solution(1190593118334199304)
XLA Ops:
  0.0 74.8 %shard_map.64 = f32[1,4,256,256]{3,2,1,0:T(8,128)} custom-call(bf16[128,1024]{1,0:T(8,128)(2,1)} %x_hbm.1, bf16[128,1024]{1,0:T(8,128)(2,1)} %dy_hbm.1, bf16[16,256,256]{2,1,0:T(8,128)(2,1)} %adj_hbm.1, s32[8]{0:T(128)} %cnt_hbm.1, s32[8,16]{1,0:T(8,128)} %trow_hbm.1, s32[8,16]{1,0:T(8,128)} %tcol_hbm.1), custom_call_target="tpu_custom_call" | custom-call | tf_op jit(solution)/shard_map/pallas_call | solution.py:577
  74.8 2.3 %copy.8 = f32[1,4,256,256]{3,2,1,0:T(8,128)} copy(f32[1,4,256,256]{3,2,1,0:T(8,128)} %shard_map.64) | data formatting | bytes 2097152

commit v4 on v3

--- a/solution.py
+++ b/solution.py
@@ -122,7 +122,8 @@
     tcol,
     gtab,
     xbuf,
-    hbuf,
+    hbuf_a,
+    hbuf_b,
     adj,
     dyt,
     dy_t,
@@ -213,7 +214,9 @@
     for c in x_local:
         c.wait()
     xg = Gather(rows, tiles, xbuf, xs_sem, xr_sem, d, me)
-    hg = Gather(rows, tiles, hbuf, hs_sem, hr_sem, d, me)
+    hbuf = (hbuf_a, hbuf_b)
+    hg = [Gather(rows, tiles, hbuf[c], hs_sem.at[c], hr_sem.at[c], d, me) for c in range(2)]
+    half = tile // 2
     xg.start()
     for c in table_local + dy_local + [adj_local]:
         c.wait()
@@ -337,28 +340,29 @@
 
     lax.fori_loop(0, slots // group, h_body, 0)
 
+    @pl.when(is_end)
+    def _():
+        x_feat().start()
+
     chunk = min(32, feat)
 
-    def h_sum(c, carry):
-        at = pl.ds(pl.multiple_of(c * chunk, chunk), chunk)
-        total = [jnp.zeros((chunk, tile), F32) for _ in range(tiles)]
+    def h_sum(c, n, carry):
+        at = pl.ds(pl.multiple_of(n * chunk, chunk), chunk)
+        total = [jnp.zeros((chunk, half), F32) for _ in range(tiles)]
         for s in range(slots):
-            term = terms[s, at, :]
+            term = terms[s, at, c * half : (c + 1) * half]
             row = jnp.where(s < my_count, trow[me, s], -1)
             for i in range(tiles):
                 total[i] = total[i] + jnp.where(row == i, term, 0.0)
         for i in range(tiles):
-            hbuf[me * tiles + i, at, :] = total[i].astype(BF16)
-        return carry
-
-    lax.fori_loop(0, feat // chunk, h_sum, 0)
-    hg.start()
-
-    @pl.when(is_end)
-    def _():
-        x_feat().start()
-
-    hg.forward(1, rows // 4)
+            hbuf[c][me * tiles + i, at, :] = total[i].astype(BF16)
+        return carry
+
+    for c in range(2):
+        lax.fori_loop(0, feat // chunk, functools.partial(h_sum, c), 0)
+        hg[c].start()
+        hg[c].forward(1, rows // 4)
+
     for t in range(1, rows):
         g_copy(t).wait_recv()
 
@@ -375,20 +379,20 @@
     def _():
         g_feat().start()
 
-    hg.forward(rows // 4, rows)
+    hg[0].forward(rows // 4, rows)
 
     def up_slot(n):
         return (last_d - n // share) * share + n % share
 
-    def h_send(n, carry):
+    def h_send(c, n, carry):
         s = jnp.where(d == 0, up_slot(n), n)
-        hpick[s] = hbuf[tcol[me, s]]
-        h_feat(s).start()
+        hpick[c * slots + s] = hbuf[c][tcol[me, s]]
+        h_feat(c * slots + s).start()
         return carry
 
     @pl.when(is_end)
     def _():
-        lax.fori_loop(0, kept, h_send, 0)
+        lax.fori_loop(0, kept, functools.partial(h_send, 0), 0)
 
     @pl.when(is_next)
     def _():
@@ -404,14 +408,16 @@
     def live(s, p):
         return jnp.where(s < my_count, p, 0.0)
 
-    def partial(s):
+    def partial(s, c):
         row = trow[me, s]
         col = tcol[me, s]
-        return live(s, dots(dy_t[row], g_t[row], hbuf[col], xbuf[col]))
-
-    def partial_end(s):
+        x = xbuf[col, :, c * half : (c + 1) * half]
+        return live(s, dots(dy_t[row], g_t[row], hbuf[c][col], x))
+
+    def partial_end(s, c):
         row = trow[me, s]
-        return live(s, dots(dy_t2[row], g_t2[row], h2[s], x2[s]))
+        x = x2[s, :, c * half : (c + 1) * half]
+        return live(s, dots(dy_t2[row], g_t2[row], h2[c * slots + s], x))
 
     def up_copy(s):
         return pltpu.make_async_remote_copy(
@@ -433,103 +439,125 @@
             device_id_type=MESH,
         )
 
-    def up_step(n):
+    def up_step(n, c):
         s = up_slot(n)
+        at = c * slots + s
 
         @pl.when((d == 1) & (n < (last_d - 1) * share))
         def _():
-            p = partial(s)
-            h_feat(s).wait_recv()
-            send_up[s] = (p + partial_end(s)).astype(BF16)
-            up_copy(s).start()
+            p = partial(s, c)
+            h_feat(at).wait_recv()
+            send_up[at] = (p + partial_end(s, c)).astype(BF16)
+            up_copy(at).start()
 
         @pl.when((d > 1) & (d < last_d) & (n < (last_d - d) * share))
         def _():
-            p = partial(s)
-            up_copy(s).wait_recv()
-            send_up[s] = (p + recv_up[s].astype(F32)).astype(BF16)
-            up_copy(s).start()
-
-    def dn_step(n):
+            p = partial(s, c)
+            up_copy(at).wait_recv()
+            send_up[at] = (p + recv_up[at].astype(F32)).astype(BF16)
+            up_copy(at).start()
+
+    def dn_step(n, c):
+        at = c * slots + n
+
         @pl.when((d == last_d - 1) & (n < d * share))
         def _():
-            p = partial(n)
-            h_feat(n).wait_recv()
-            send_dn[n] = (p + partial_end(n)).astype(BF16)
-            dn_copy(n).start()
+            p = partial(n, c)
+            h_feat(at).wait_recv()
+            send_dn[at] = (p + partial_end(n, c)).astype(BF16)
+            dn_copy(at).start()
 
         @pl.when((d > 0) & (d < last_d - 1) & (n < d * share))
         def _():
-            p = partial(n)
-            dn_copy(n).wait_recv()
-            send_dn[n] = (p + recv_dn[n].astype(F32)).astype(BF16)
-            dn_copy(n).start()
+            p = partial(n, c)
+            dn_copy(at).wait_recv()
+            send_dn[at] = (p + recv_dn[at].astype(F32)).astype(BF16)
+            dn_copy(at).start()
 
     lag = 1
 
-    def z_body(n, carry):
+    def z_body(c, n, carry):
         @pl.when(d < last_d - 1)
         def _():
-            up_step(n)
+            up_step(n, c)
 
             @pl.when(n >= lag)
             def _():
-                dn_step(n - lag)
+                dn_step(n - lag, c)
 
         @pl.when(d == last_d - 1)
         def _():
-            dn_step(n)
+            dn_step(n, c)
 
             @pl.when(n >= lag)
             def _():
-                up_step(n - lag)
-
-        return carry
-
-    @pl.when((d > 0) & (d < last_d))
-    def _():
-        lax.fori_loop(0, (last_d - 1) * share + lag, z_body, 0)
-
-    def own_first(k, carry):
-        out[k] = partial(d * share + k)
-        return carry
-
-    lax.fori_loop(0, share, own_first, 0)
-
-    def own_end(k, carry):
-        s = d * share + k
-        h_feat(s).wait_recv()
-        out[k] += partial_end(s)
-        return carry
-
-    @pl.when(is_next)
-    def _():
-        lax.fori_loop(0, share, own_end, 0)
-
-    def own_up(k, carry):
-        s = d * share + k
-        up_copy(s).wait_recv()
-        out[k] += recv_up[s].astype(F32)
-        return carry
-
-    def own_dn(k, carry):
-        s = d * share + k
-        dn_copy(s).wait_recv()
-        out[k] += recv_dn[s].astype(F32)
-        return carry
-
-    @pl.when(d >= 2)
-    def _():
-        lax.fori_loop(0, share, own_up, 0)
-
-    @pl.when(d <= last_d - 2)
-    def _():
-        lax.fori_loop(0, share, own_dn, 0)
+                up_step(n - lag, c)
+
+        return carry
+
+    z_end = (last_d - 1) * share + lag
+    z_mid = z_end // 2
+    is_inner = (d > 0) & (d < last_d)
+
+    @pl.when(is_inner)
+    def _():
+        lax.fori_loop(0, z_mid, functools.partial(z_body, 0), 0)
+
+    hg[1].forward(rows // 4, rows)
+
+    @pl.when(is_end)
+    def _():
+        lax.fori_loop(0, kept, functools.partial(h_send, 1), 0)
+
+    @pl.when(is_inner)
+    def _():
+        lax.fori_loop(z_mid, z_end, functools.partial(z_body, 0), 0)
+        lax.fori_loop(0, z_end, functools.partial(z_body, 1), 0)
+
+    for c in range(2):
+        cols = slice(c * half, (c + 1) * half)
+
+        def own_first(k, carry):
+            out[k, :, cols] = partial(d * share + k, c)
+            return carry
+
+        def own_end(k, carry):
+            s = d * share + k
+            h_feat(c * slots + s).wait_recv()
+            out[k, :, cols] += partial_end(s, c)
+            return carry
+
+        def own_up(k, carry):
+            at = c * slots + d * share + k
+            up_copy(at).wait_recv()
+            out[k, :, cols] += recv_up[at].astype(F32)
+            return carry
+
+        def own_dn(k, carry):
+            at = c * slots + d * share + k
+            dn_copy(at).wait_recv()
+            out[k, :, cols] += recv_dn[at].astype(F32)
+            return carry
+
+        lax.fori_loop(0, share, own_first, 0)
+
+        @pl.when(is_next)
+        def _():
+            lax.fori_loop(0, share, own_end, 0)
+
+        @pl.when(d >= 2)
+        def _():
+            lax.fori_loop(0, share, own_up, 0)
+
+        @pl.when(d <= last_d - 2)
+        def _():
+            lax.fori_loop(0, share, own_dn, 0)
 
     result = pltpu.make_async_copy(out, out_hbm.at[0], local_sem.at[2 * tiles + 4])
     result.start()
     xg.drain()
-    hg.drain()
+    hg[0].drain()
+    hg[1].drain()
     for t in range(1, rows):
         g_copy(t).wait_send()
 
@@ -541,6 +569,7 @@
 
         def h_drain(n, carry):
             h_feat(low + n).wait_send()
+            h_feat(slots + low + n).wait_send()
             return carry
 
         lax.fori_loop(0, kept, h_drain, 0)
@@ -548,13 +577,15 @@
     def z_drain(s, carry):
         t = s // share
 
-        @pl.when((d > 0) & (d < last_d) & (t > d))
+        @pl.when(is_inner & (t > d))
         def _():
             up_copy(s).wait_send()
-
-        @pl.when((d > 0) & (d < last_d) & (t < d))
+            up_copy(slots + s).wait_send()
+
+        @pl.when(is_inner & (t < d))
         def _():
             dn_copy(s).wait_send()
+            dn_copy(slots + s).wait_send()
 
         return carry
 
@@ -570,10 +601,10 @@
     dma = pltpu.SemaphoreType.DMA
     hbm = pl.BlockSpec(memory_space=pltpu.HBM)
     ntiles = rows * tiles
-    node = pltpu.VMEM((ntiles, feat, tile), BF16)
     turned = pltpu.VMEM((tiles, tile, feat), BF16)
     picked = pltpu.VMEM((slots, feat, tile), BF16)
-    sums = pltpu.VMEM((slots, tile, tile), BF16)
+    picked_half = pltpu.VMEM((2 * slots, feat, tile // 2), BF16)
+    sums = pltpu.VMEM((2 * slots, tile, tile // 2), BF16)
     return pl.pallas_call(
         functools.partial(kernel, rows, depth),
         out_shape=jax.ShapeDtypeStruct((1, share, tile, tile), F32),
@@ -585,18 +616,19 @@
             pltpu.SMEM(tile_row.shape, jnp.int32),
             pltpu.SMEM(tile_col.shape, jnp.int32),
             pltpu.SMEM((rows * tiles,), jnp.int32),
-            node,
-            node,
-            sums,
+            pltpu.VMEM((ntiles, feat, tile), BF16),
+            pltpu.VMEM((ntiles, feat, tile // 2), BF16),
+            pltpu.VMEM((ntiles, feat, tile // 2), BF16),
+            pltpu.VMEM((slots, tile, tile), BF16),
             pltpu.VMEM((tiles, feat, tile), BF16),
             turned,
             turned,
             turned,
             turned,
             picked,
+            picked_half,
             picked,
-            picked,
-            picked,
+            picked_half,
             pltpu.VMEM((slots, feat, tile), F32),
             picked,
             pltpu.VMEM((rows, 2, feat, tile), BF16),
@@ -609,21 +641,21 @@
             dma((2 * tiles + 5,)),
             dma((2 * rows,)),
             dma((2 * rows,)),
-            dma((2 * rows,)),
-            dma((2 * rows,)),
+            dma((2, 2 * rows)),
+            dma((2, 2 * rows)),
             dma((rows,)),
             dma((rows,)),
-            dma((slots,)),
-            dma((slots,)),
-            dma((slots,)),
-            dma((slots,)),
+            dma((2 * slots,)),
+            dma((2 * slots,)),
+            dma((2 * slots,)),
+            dma((2 * slots,)),
             dma((3,)),
             dma((3,)),
-            dma((slots,)),
-            dma((slots,)),
+            dma((2 * slots,)),
+            dma((2 * slots,)),
         ],
         compiler_params=pltpu.CompilerParams(
-            collective_id=0, has_side_effects=True, vmem_limit_bytes=64 * 1024 * 1024
+            collective_id=0, has_side_effects=True, vmem_limit_bytes=62 * 1024 * 1024 + 960 * 1024
         ),
     )(node_feat, grad_out, adjacency, tile_count, tile_row, tile_col)
 

time: 78.2 us -> 82.3 us (1.052); the launches traced: 77.1 us -> 82.1 us
  Pallas kernels: 74.8 us -> 79.8 us
    pallas_call x1, Pallas kernels: 74.8 us -> 79.8 us  [body(): pl.pallas_call(functools.partial(kernel, rows, depth), out_shape=jax.Shap...]
where the time goes in v4:
time: 82.3 us; the launch traced here: 82.1 us
  Pallas kernels  79.8 us (97%)
  local copies, waits for them, and re-layouts  2.29 us (3%)
    pallas_call x1, Pallas kernels, body(): pl.pallas_call(functools.partial(kernel, rows, depth), out_shape=jax.Shap...  79.8 us
    unnamed x1, local copies, waits for them, and re-layouts  2.29 us

profile of v4, /device:TPU:18, one launch (start us, length us, event | category | flops | bytes accessed | tf_op | source)
XLA Modules:
  0.0 82.1 jit_solution(3041396295430642549)
XLA Ops:
  0.0 79.8 %shard_map.64 = f32[1,4,256,256]{3,2,1,0:T(8,128)} custom-call(bf16[128,1024]{1,0:T(8,128)(2,1)} %x_hbm.1, bf16[128,1024]{1,0:T(8,128)(2,1)} %dy_hbm.1, bf16[16,256,256]{2,1,0:T(8,128)(2,1)} %adj_hbm.1, s32[8]{0:T(128)} %cnt_hbm.1, s32[8,16]{1,0:T(8,128)} %trow_hbm.1, s32[8,16]{1,0:T(8,128)} %tcol_hbm.1), custom_call_target="tpu_custom_call" | custom-call | tf_op jit(solution)/shard_map/pallas_call | solution.py:608
  79.8 2.3 %copy.8 = f32[1,4,256,256]{3,2,1,0:T(8,128)} copy(f32[1,4,256,256]{3,2,1,0:T(8,128)} %shard_map.64) | data formatting | bytes 2097152

commit v5 on v4

--- a/solution.py
+++ b/solution.py
@@ -6,6 +6,8 @@
 from jax.experimental import pallas as pl
 from jax.experimental.pallas import tpu as pltpu
 from jax.sharding import PartitionSpec as P
+
+PIECES = 1
 
 MESH = pl.DeviceIdType.MESH
 F32 = jnp.float32
@@ -122,8 +124,7 @@
     tcol,
     gtab,
     xbuf,
-    hbuf_a,
-    hbuf_b,
+    hbuf,
     adj,
     dyt,
     dy_t,
@@ -197,13 +198,16 @@
             barrier, inc=1, device_id=((d + t) % depth, me), device_id_type=MESH
         )
 
-    @pl.when(d <= 1)
-    def _():
-        recv_up[...] = jnp.zeros_like(recv_up)
-
-    @pl.when(d >= last_d - 1)
-    def _():
-        recv_dn[...] = jnp.zeros_like(recv_dn)
+    for c in range(PIECES):
+        at = pl.ds(c * slots + d * share, share)
+
+        @pl.when(d <= 1)
+        def _():
+            recv_up[at] = jnp.zeros((share,) + recv_up.shape[1:], BF16)
+
+        @pl.when(d >= last_d - 1)
+        def _():
+            recv_dn[at] = jnp.zeros((share,) + recv_dn.shape[1:], BF16)
 
     for t in range(rows):
         gin[t, 2] = jnp.zeros((feat, tile), BF16)
@@ -214,9 +218,10 @@
     for c in x_local:
         c.wait()
     xg = Gather(rows, tiles, xbuf, xs_sem, xr_sem, d, me)
-    hbuf = (hbuf_a, hbuf_b)
-    hg = [Gather(rows, tiles, hbuf[c], hs_sem.at[c], hr_sem.at[c], d, me) for c in range(2)]
-    half = tile // 2
+    hg = [
+        Gather(rows, tiles, hbuf[c], hs_sem.at[c], hr_sem.at[c], d, me) for c in range(PIECES)
+    ]
+    half = tile // PIECES
     xg.start()
     for c in table_local + dy_local + [adj_local]:
         c.wait()
@@ -358,7 +363,7 @@
             hbuf[c][me * tiles + i, at, :] = total[i].astype(BF16)
         return carry
 
-    for c in range(2):
+    for c in range(PIECES):
         lax.fori_loop(0, feat // chunk, functools.partial(h_sum, c), 0)
         hg[c].start()
         hg[c].forward(1, rows // 4)
@@ -400,24 +405,20 @@
         x_feat().wait_recv()
         g_feat().wait_recv()
 
-    def dots(dy, g, h, x):
-        lhs = jnp.concatenate([dy, g], axis=1)
-        rhs = jnp.concatenate([h, x], axis=0)
-        return jnp.dot(lhs, rhs, preferred_element_type=F32)
-
-    def live(s, p):
-        return jnp.where(s < my_count, p, 0.0)
-
-    def partial(s, c):
+    def partial(s, c, with_end=False):
         row = trow[me, s]
         col = tcol[me, s]
-        x = xbuf[col, :, c * half : (c + 1) * half]
-        return live(s, dots(dy_t[row], g_t[row], hbuf[c][col], x))
-
-    def partial_end(s, c):
-        row = trow[me, s]
-        x = x2[s, :, c * half : (c + 1) * half]
-        return live(s, dots(dy_t2[row], g_t2[row], h2[c * slots + s], x))
+        cols = slice(c * half, (c + 1) * half)
+        lhs = [dy_t[row], g_t[row]]
+        rhs = [hbuf[c][col], xbuf[col, :, cols]]
+        if with_end:
+            lhs += [dy_t2[row], g_t2[row]]
+            rhs += [h2[c * slots + s], x2[s, :, cols]]
+        return jnp.dot(
+            jnp.concatenate(lhs, axis=1),
+            jnp.concatenate(rhs, axis=0),
+            preferred_element_type=F32,
+        )
 
     def up_copy(s):
         return pltpu.make_async_remote_copy(
@@ -445,9 +446,8 @@
 
         @pl.when((d == 1) & (n < (last_d - 1) * share))
         def _():
-            p = partial(s, c)
             h_feat(at).wait_recv()
-            send_up[at] = (p + partial_end(s, c)).astype(BF16)
+            send_up[at] = partial(s, c, True).astype(BF16)
             up_copy(at).start()
 
         @pl.when((d > 1) & (d < last_d) & (n < (last_d - d) * share))
@@ -462,9 +462,8 @@
 
         @pl.when((d == last_d - 1) & (n < d * share))
         def _():
-            p = partial(n, c)
             h_feat(at).wait_recv()
-            send_dn[at] = (p + partial_end(n, c)).astype(BF16)
+            send_dn[at] = partial(n, c, True).astype(BF16)
             dn_copy(at).start()
 
         @pl.when((d > 0) & (d < last_d - 1) & (n < d * share))
@@ -476,6 +475,22 @@
 
     lag = 1
 
+    z_end = (last_d - 1) * share + lag
+    is_inner = (d > 0) & (d < last_d)
+
+    def own_step(k, c):
+        s = d * share + k
+        cols = slice(c * half, (c + 1) * half)
+
+        @pl.when(is_next)
+        def _():
+            h_feat(c * slots + s).wait_recv()
+            out[k, :, cols] = partial(s, c, True)
+
+        @pl.when((d != 1) & (d != last_d - 1))
+        def _():
+            out[k, :, cols] = partial(s, c)
+
     def z_body(c, n, carry):
         @pl.when(d < last_d - 1)
         def _():
@@ -493,71 +508,64 @@
             def _():
                 up_step(n - lag, c)
 
-        return carry
-
-    z_end = (last_d - 1) * share + lag
-    z_mid = z_end // 2
-    is_inner = (d > 0) & (d < last_d)
-
-    @pl.when(is_inner)
-    def _():
-        lax.fori_loop(0, z_mid, functools.partial(z_body, 0), 0)
-
-    hg[1].forward(rows // 4, rows)
-
-    @pl.when(is_end)
-    def _():
-        lax.fori_loop(0, kept, functools.partial(h_send, 1), 0)
-
-    @pl.when(is_inner)
-    def _():
-        lax.fori_loop(z_mid, z_end, functools.partial(z_body, 0), 0)
-        lax.fori_loop(0, z_end, functools.partial(z_body, 1), 0)
-
-    for c in range(2):
-        cols = slice(c * half, (c + 1) * half)
-
-        def own_first(k, carry):
-            out[k, :, cols] = partial(d * share + k, c)
-            return carry
-
-        def own_end(k, carry):
-            s = d * share + k
-            h_feat(c * slots + s).wait_recv()
-            out[k, :, cols] += partial_end(s, c)
-            return carry
-
-        def own_up(k, carry):
-            at = c * slots + d * share + k
-            up_copy(at).wait_recv()
-            out[k, :, cols] += recv_up[at].astype(F32)
-            return carry
-
-        def own_dn(k, carry):
-            at = c * slots + d * share + k
-            dn_copy(at).wait_recv()
-            out[k, :, cols] += recv_dn[at].astype(F32)
-            return carry
-
-        lax.fori_loop(0, share, own_first, 0)
-
-        @pl.when(is_next)
-        def _():
-            lax.fori_loop(0, share, own_end, 0)
-
-        @pl.when(d >= 2)
-        def _():
-            lax.fori_loop(0, share, own_up, 0)
-
-        @pl.when(d <= last_d - 2)
-        def _():
-            lax.fori_loop(0, share, own_dn, 0)
-
-    result = pltpu.make_async_copy(out, out_hbm.at[0], local_sem.at[2 * tiles + 4])
-    result.start()
+        @pl.when(n >= z_end - share)
+        def _():
+            own_step(n - (z_end - share), c)
+
+        return carry
+
+    def z_range(c, begin, end):
+        @pl.when(is_inner)
+        def _():
+            lax.fori_loop(begin, end, functools.partial(z_body, c), 0)
+
+    def own_range(c):
+        @pl.when(is_end)
+        def _():
+            lax.fori_loop(0, share, lambda k, carry: (own_step(k, c), carry)[1], 0)
+
+    for c in range(PIECES):
+        z_mid = z_end // 2 if c + 1 < PIECES else z_end
+        z_range(c, 0, z_mid)
+        own_range(c)
+        if c + 1 < PIECES:
+            hg[c + 1].forward(rows // 4, rows)
+
+            @pl.when(is_end)
+            def _():
+                lax.fori_loop(0, kept, functools.partial(h_send, c + 1), 0)
+
+        z_range(c, z_mid, z_end)
+
+    def result_copy(k):
+        return pltpu.make_async_copy(
+            out.at[k], out_hbm.at[0, k], local_sem.at[2 * tiles + 4 + k]
+        )
+
+    def finish(k, carry):
+        s = d * share + k
+        for c in range(PIECES):
+            at = c * slots + s
+            cols = slice(c * half, (c + 1) * half)
+
+            @pl.when(d >= 2)
+            def _():
+                up_copy(at).wait_recv()
+
+            @pl.when(d <= last_d - 2)
+            def _():
+                dn_copy(at).wait_recv()
+
+            total = out[k, :, cols] + recv_up[at].astype(F32) + recv_dn[at].astype(F32)
+            out[k, :, cols] = jnp.where(s < my_count, total, 0.0)
+        result_copy(k).start()
+        return carry
+
+    lax.fori_loop(0, share, finish, 0)
+
     xg.drain()
-    hg[0].drain()
-    hg[1].drain()
+    for c in range(PIECES):
+        hg[c].drain()
     for t in range(1, rows):
         g_copy(t).wait_send()
 
@@ -568,8 +576,8 @@
         g_feat().wait_send()
 
         def h_drain(n, carry):
-            h_feat(low + n).wait_send()
-            h_feat(slots + low + n).wait_send()
+            for c in range(PIECES):
+                h_feat(c * slots + low + n).wait_send()
             return carry
 
         lax.fori_loop(0, kept, h_drain, 0)
@@ -579,18 +587,19 @@
 
         @pl.when(is_inner & (t > d))
         def _():
-            up_copy(s).wait_send()
-            up_copy(slots + s).wait_send()
+            for c in range(PIECES):
+                up_copy(c * slots + s).wait_send()
 
         @pl.when(is_inner & (t < d))
         def _():
-            dn_copy(s).wait_send()
-            dn_copy(slots + s).wait_send()
+            for c in range(PIECES):
+                dn_copy(c * slots + s).wait_send()
 
         return carry
 
     lax.fori_loop(0, slots, z_drain, 0)
-    result.wait()
+    for k in range(share):
+        result_copy(k).wait()
 
 
 def body(rows, depth, node_feat, grad_out, adjacency, tile_count, tile_row, tile_col):
@@ -603,8 +612,8 @@
     ntiles = rows * tiles
     turned = pltpu.VMEM((tiles, tile, feat), BF16)
     picked = pltpu.VMEM((slots, feat, tile), BF16)
-    picked_half = pltpu.VMEM((2 * slots, feat, tile // 2), BF16)
-    sums = pltpu.VMEM((2 * slots, tile, tile // 2), BF16)
+    picked_half = pltpu.VMEM((PIECES * slots, feat, tile // PIECES), BF16)
+    sums = pltpu.VMEM((PIECES * slots, tile, tile // PIECES), BF16)
     return pl.pallas_call(
         functools.partial(kernel, rows, depth),
         out_shape=jax.ShapeDtypeStruct((1, share, tile, tile), F32),
@@ -617,8 +626,7 @@
             pltpu.SMEM(tile_col.shape, jnp.int32),
             pltpu.SMEM((rows * tiles,), jnp.int32),
             pltpu.VMEM((ntiles, feat, tile), BF16),
-            pltpu.VMEM((ntiles, feat, tile // 2), BF16),
-            pltpu.VMEM((ntiles, feat, tile // 2), BF16),
+            [pltpu.VMEM((ntiles, feat, tile // PIECES), BF16)] * PIECES,
             pltpu.VMEM((slots, tile, tile), BF16),
             pltpu.VMEM((tiles, feat, tile), BF16),
             turned,
@@ -638,24 +646,24 @@
             sums,
             sums,
             sums,
-            dma((2 * tiles + 5,)),
+            dma((2 * tiles + 4 + share,)),
             dma((2 * rows,)),
             dma((2 * rows,)),
-            dma((2, 2 * rows)),
-            dma((2, 2 * rows)),
+            dma((PIECES, 2 * rows)),
+            dma((PIECES, 2 * rows)),
             dma((rows,)),
             dma((rows,)),
-            dma((2 * slots,)),
-            dma((2 * slots,)),
-            dma((2 * slots,)),
-            dma((2 * slots,)),
+            dma((PIECES * slots,)),
+            dma((PIECES * slots,)),
+            dma((PIECES * slots,)),
+            dma((PIECES * slots,)),
             dma((3,)),
             dma((3,)),
-            dma((2 * slots,)),
-            dma((2 * slots,)),
+            dma((PIECES * slots,)),
+            dma((PIECES * slots,)),
         ],
         compiler_params=pltpu.CompilerParams(
-            collective_id=0, has_side_effects=True, vmem_limit_bytes=62 * 1024 * 1024 + 960 * 1024
+            collective_id=0, has_side_effects=True, vmem_limit_bytes=64 * 1024 * 1024
         ),
     )(node_feat, grad_out, adjacency, tile_count, tile_row, tile_col)
 

time: 82.3 us -> 77.2 us (0.938)
  Pallas kernels: 79.8 us -> 73.9 us
    pallas_call x1, Pallas kernels: 79.8 us -> 73.9 us  [body(): pl.pallas_call(functools.partial(kernel, rows, depth), out_shape=jax.Shap...]
where the time goes in v5:
time: 77.2 us; the launch traced here: 76.2 us
  Pallas kernels  73.9 us (96%)
  local copies, waits for them, and re-layouts  2.29 us (3%)
    pallas_call x1, Pallas kernels, body(): pl.pallas_call(functools.partial(kernel, rows, depth), out_shape=jax.Shap...  73.9 us
    unnamed x1, local copies, waits for them, and re-layouts  2.29 us

profile of v5, /device:TPU:18, one launch (start us, length us, event | category | flops | bytes accessed | tf_op | source)
XLA Modules:
  0.0 76.2 jit_solution(12623560586559537421)
XLA Ops:
  0.0 73.9 %shard_map.64 = f32[1,4,256,256]{3,2,1,0:T(8,128)} custom-call(bf16[128,1024]{1,0:T(8,128)(2,1)} %x_hbm.1, bf16[128,1024]{1,0:T(8,128)(2,1)} %dy_hbm.1, bf16[16,256,256]{2,1,0:T(8,128)(2,1)} %adj_hbm.1, s32[8]{0:T(128)} %cnt_hbm.1, s32[8,16]{1,0:T(8,128)} %trow_hbm.1, s32[8,16]{1,0:T(8,128)} %tcol_hbm.1), custom_call_target="tpu_custom_call" | custom-call | tf_op jit(solution)/shard_map/pallas_call | solution.py:617
  73.9 2.3 %copy.8 = f32[1,4,256,256]{3,2,1,0:T(8,128)} copy(f32[1,4,256,256]{3,2,1,0:T(8,128)} %shard_map.64) | data formatting | bytes 2097152

commit v6 on v5

--- a/solution.py
+++ b/solution.py
@@ -7,7 +7,7 @@
 from jax.experimental.pallas import tpu as pltpu
 from jax.sharding import PartitionSpec as P
 
-PIECES = 1
+PIECES = 2
 
 MESH = pl.DeviceIdType.MESH
 F32 = jnp.float32

time: 77.2 us -> 81.9 us (1.061); the launches traced: 76.2 us -> 81.8 us
  Pallas kernels: 73.9 us -> 79.5 us
    pallas_call x1, Pallas kernels: 73.9 us -> 79.5 us  [body(): pl.pallas_call(functools.partial(kernel, rows, depth), out_shape=jax.Shap...]
where the time goes in v6:
time: 81.9 us; the launch traced here: 81.8 us
  Pallas kernels  79.5 us (97%)
  local copies, waits for them, and re-layouts  2.29 us (3%)
    pallas_call x1, Pallas kernels, body(): pl.pallas_call(functools.partial(kernel, rows, depth), out_shape=jax.Shap...  79.5 us
    unnamed x1, local copies, waits for them, and re-layouts  2.29 us

profile of v6, /device:TPU:18, one launch (start us, length us, event | category | flops | bytes accessed | tf_op | source)
XLA Modules:
  0.0 81.8 jit_solution(10047750768376043626)
XLA Ops:
  0.0 79.5 %shard_map.64 = f32[1,4,256,256]{3,2,1,0:T(8,128)} custom-call(bf16[128,1024]{1,0:T(8,128)(2,1)} %x_hbm.1, bf16[128,1024]{1,0:T(8,128)(2,1)} %dy_hbm.1, bf16[16,256,256]{2,1,0:T(8,128)(2,1)} %adj_hbm.1, s32[8]{0:T(128)} %cnt_hbm.1, s32[8,16]{1,0:T(8,128)} %trow_hbm.1, s32[8,16]{1,0:T(8,128)} %tcol_hbm.1), custom_call_target="tpu_custom_call" | custom-call | tf_op jit(solution)/shard_map/pallas_call | solution.py:617
  79.5 2.3 %copy.8 = f32[1,4,256,256]{3,2,1,0:T(8,128)} copy(f32[1,4,256,256]{3,2,1,0:T(8,128)} %shard_map.64) | data formatting | bytes 2097152

commit v7 on v5

--- a/solution.py
+++ b/solution.py
@@ -8,6 +8,7 @@
 from jax.sharding import PartitionSpec as P
 
 PIECES = 1
+WINDOW = 2
 
 MESH = pl.DeviceIdType.MESH
 F32 = jnp.float32
@@ -274,8 +275,11 @@
     inner = jnp.where(d < 2, 1 - d, 2 * last_d - 1 - d)
     inner = jnp.where(d < 2, inner, jnp.where(d >= last_d - 1, inner, 0))
     end_id = (inner, me)
-    kept = (depth - 1) * share
-    low = jnp.where(d < 2, share, 0)
+    passed = (depth - 2) * share
+    kept = passed + share
+    low = jnp.where(d < 2, 2 * share, 0)
+    next_low = jnp.where(d < 2, share, passed)
+    window = min(WINDOW, passed)
 
     def feat_copy(src, dst, n):
         return pltpu.make_async_remote_copy(
@@ -291,8 +295,12 @@
         return feat_copy(dy_t, dy_t2, 0)
 
     def x_feat():
-        at = pl.ds(low, kept)
+        at = pl.ds(low, passed)
         return feat_copy(xpick.at[at], x2.at[at], 1)
+
+    def x_next_feat():
+        at = pl.ds(next_low, share)
+        return feat_copy(xpick.at[at], x2.at[at], 3)
 
     def g_feat():
         return feat_copy(g_t, g_t2, 2)
@@ -389,15 +397,29 @@
     def up_slot(n):
         return (last_d - n // share) * share + n % share
 
+    def end_slot(n):
+        return jnp.where(d == 0, up_slot(n), n)
+
     def h_send(c, n, carry):
-        s = jnp.where(d == 0, up_slot(n), n)
+        s = end_slot(n)
         hpick[c * slots + s] = hbuf[c][tcol[me, s]]
+
+        @pl.when(n >= window)
+        def _():
+            h_feat(c * slots + end_slot(n - window)).wait_send()
+
         h_feat(c * slots + s).start()
         return carry
+
+    def h_send_all(c):
+        lax.fori_loop(0, passed, functools.partial(h_send, c), 0)
+        if c == 0:
+            x_next_feat().start()
+        lax.fori_loop(passed, kept, functools.partial(h_send, c), 0)
 
     @pl.when(is_end)
     def _():
-        lax.fori_loop(0, kept, functools.partial(h_send, 0), 0)
+        h_send_all(0)
 
     @pl.when(is_next)
     def _():
@@ -448,6 +470,11 @@
         def _():
             h_feat(at).wait_recv()
             send_up[at] = partial(s, c, True).astype(BF16)
+
+            @pl.when(n >= window)
+            def _():
+                up_copy(c * slots + up_slot(n - window)).wait_send()
+
             up_copy(at).start()
 
         @pl.when((d > 1) & (d < last_d) & (n < (last_d - d) * share))
@@ -464,6 +491,11 @@
         def _():
             h_feat(at).wait_recv()
             send_dn[at] = partial(n, c, True).astype(BF16)
+
+            @pl.when(n >= window)
+            def _():
+                dn_copy(at - window).wait_send()
+
             dn_copy(at).start()
 
         @pl.when((d > 0) & (d < last_d - 1) & (n < d * share))
@@ -484,6 +516,12 @@
 
         @pl.when(is_next)
         def _():
+            if c == 0:
+
+                @pl.when(k == 0)
+                def _():
+                    x_next_feat().wait_recv()
+
             h_feat(c * slots + s).wait_recv()
             out[k, :, cols] = partial(s, c, True)
 
@@ -533,7 +571,7 @@
 
             @pl.when(is_end)
             def _():
-                lax.fori_loop(0, kept, functools.partial(h_send, c + 1), 0)
+                h_send_all(c + 1)
 
         z_range(c, z_mid, z_end)
 
@@ -575,22 +613,31 @@
         x_feat().wait_send()
         g_feat().wait_send()
 
-        def h_drain(n, carry):
-            for c in range(PIECES):
-                h_feat(c * slots + low + n).wait_send()
-            return carry
-
-        lax.fori_loop(0, kept, h_drain, 0)
+        x_next_feat().wait_send()
+        for c in range(PIECES):
+            for n in range(kept - window, kept):
+                h_feat(c * slots + end_slot(n)).wait_send()
+
+    for c in range(PIECES):
+        for n in range(passed - window, passed):
+
+            @pl.when(d == 1)
+            def _():
+                up_copy(c * slots + up_slot(n)).wait_send()
+
+            @pl.when(d == last_d - 1)
+            def _():
+                dn_copy(c * slots + n).wait_send()
 
     def z_drain(s, carry):
         t = s // share
 
-        @pl.when(is_inner & (t > d))
+        @pl.when((d > 1) & (d < last_d) & (t > d))
         def _():
             for c in range(PIECES):
                 up_copy(c * slots + s).wait_send()
 
-        @pl.when(is_inner & (t < d))
+        @pl.when((d > 0) & (d < last_d - 1) & (t < d))
         def _():
             for c in range(PIECES):
                 dn_copy(c * slots + s).wait_send()
@@ -657,8 +704,8 @@
             dma((PIECES * slots,)),
             dma((PIECES * slots,)),
             dma((PIECES * slots,)),
-            dma((3,)),
-            dma((3,)),
+            dma((4,)),
+            dma((4,)),
             dma((PIECES * slots,)),
             dma((PIECES * slots,)),
         ],

time: 77.2 us -> 71.7 us (0.929)
  Pallas kernels: 73.9 us -> 68.6 us
    pallas_call x1, Pallas kernels: 73.9 us -> 68.6 us  [body(): pl.pallas_call(functools.partial(kernel, rows, depth), out_shape=jax.Shap...]
where the time goes in v7:
time: 71.7 us; the launch traced here: 70.9 us
  Pallas kernels  68.6 us (96%)
  local copies, waits for them, and re-layouts  2.29 us (3%)
    pallas_call x1, Pallas kernels, body(): pl.pallas_call(functools.partial(kernel, rows, depth), out_shape=jax.Shap...  68.6 us
    unnamed x1, local copies, waits for them, and re-layouts  2.29 us

profile of v7, /device:TPU:18, one launch (start us, length us, event | category | flops | bytes accessed | tf_op | source)
XLA Modules:
  0.0 70.9 jit_solution(9864790360090691163)
XLA Ops:
  0.0 68.6 %shard_map.64 = f32[1,4,256,256]{3,2,1,0:T(8,128)} custom-call(bf16[128,1024]{1,0:T(8,128)(2,1)} %x_hbm.1, bf16[128,1024]{1,0:T(8,128)(2,1)} %dy_hbm.1, bf16[16,256,256]{2,1,0:T(8,128)(2,1)} %adj_hbm.1, s32[8]{0:T(128)} %cnt_hbm.1, s32[8,16]{1,0:T(8,128)} %trow_hbm.1, s32[8,16]{1,0:T(8,128)} %tcol_hbm.1), custom_call_target="tpu_custom_call" | custom-call | tf_op jit(solution)/shard_map/pallas_call | solution.py:664
  68.6 2.3 %copy.8 = f32[1,4,256,256]{3,2,1,0:T(8,128)} copy(f32[1,4,256,256]{3,2,1,0:T(8,128)} %shard_map.64) | data formatting | bytes 2097152

commit v8 on v7

--- a/solution.py
+++ b/solution.py
@@ -264,7 +264,7 @@
             device_id_type=MESH,
         )
 
-    xg.forward(1, rows // 4)
+    xg.forward(1, rows // 2)
     order = sorted(range(1, rows), key=lambda t: (-bin(t // 2).count("1"), t % 2, t))
     for t in order:
         g_copy(t).start()
@@ -339,7 +339,7 @@
 
     lax.fori_loop(0, rows, g_table, 0)
 
-    xg.forward(rows // 4, rows)
+    xg.forward(rows // 2, rows)
 
     def h_body(n, carry):
         for u in range(group):

time: 71.7 us -> 69.2 us (0.965)
  the two profiles are of different devices: /device:TPU:18 before, /device:TPU:15 now
where the time goes in v8:
time: 69.2 us; the launch traced here: 69 us
  Pallas kernels  66.7 us (96%)
  local copies, waits for them, and re-layouts  2.29 us (3%)
    pallas_call x1, Pallas kernels, body(): pl.pallas_call(functools.partial(kernel, rows, depth), out_shape=jax.Shap...  66.7 us
    unnamed x1, local copies, waits for them, and re-layouts  2.29 us

profile of v8, /device:TPU:15, one launch (start us, length us, event | category | flops | bytes accessed | tf_op | source)
XLA Modules:
  0.0 69.0 jit_solution(15345719077538796658)
XLA Ops:
  0.0 66.7 %shard_map.64 = f32[1,4,256,256]{3,2,1,0:T(8,128)} custom-call(bf16[128,1024]{1,0:T(8,128)(2,1)} %x_hbm.1, bf16[128,1024]{1,0:T(8,128)(2,1)} %dy_hbm.1, bf16[16,256,256]{2,1,0:T(8,128)(2,1)} %adj_hbm.1, s32[8]{0:T(128)} %cnt_hbm.1, s32[8,16]{1,0:T(8,128)} %trow_hbm.1, s32[8,16]{1,0:T(8,128)} %tcol_hbm.1), custom_call_target="tpu_custom_call" | custom-call | tf_op jit(solution)/shard_map/pallas_call | solution.py:664
  66.7 2.3 %copy.8 = f32[1,4,256,256]{3,2,1,0:T(8,128)} copy(f32[1,4,256,256]{3,2,1,0:T(8,128)} %shard_map.64) | data formatting | bytes 2097152
